TPU v7x, 32 devices: a whole 2x2x4 slice. The times are simulated.
32 devices in a mesh: seq: 8 (over y, x, core), chan: 4 (over z).
Axes of the slice: x: 2, y: 2, z: 4, core: 2. Of those that a mesh axis runs over, the one named last changes fastest.
Arguments:
- tokens: bfloat16 [4096, 8192], P('seq'), may hold values from -6 to 6
- proj_weight: bfloat16 [8192, 3, 2048], P('seq', None, 'chan'), may hold values from -0.0625 to 0.0625
- residues: float32 [16, 2048], P(None, 'chan'), may hold values from -1.5 to 1.5
- decay_rates: float32 [16, 2048], P(None, 'chan'), may hold values from 0.00012207031 to 0.05
- skip_gain: float32 [2048], P('chan'), may hold values from -3 to 3
- grad_out: bfloat16 [4096, 2048], P('seq', 'chan'), may hold values from -6 to 6
Outputs:
- gated_output: bfloat16 [4096, 2048], P('seq', 'chan')
- grad_tokens: bfloat16 [4096, 8192], P('seq', 'chan')
All inputs are finite; a program needn't handle non-finite values.
Results may differ from a plain program's by a relative error of at most 0.022.
Values may be sent and summed in bfloat16 or wider, within the bound.
No kernel may reach another device: no remote copies, remote signals or barrier semaphores. Data moves between devices by JAX's collectives and lax.ppermute only.
A program may use at most 128 MiB of HBM per device.

v0:
```python
import functools

import jax
import jax.numpy as jnp
from jax import lax
from jax.experimental import pallas as pl
from jax.experimental.pallas import tpu as pltpu
from jax.sharding import PartitionSpec as P

LANES = 128
WIDTHS = (256, 256)
SUBS = 8
MODES = 16
BLOCKS = 8
VMEM_BYTES = 60 * 1024 * 1024


def coefficients(residues, decay_rates, rows):
    return jnp.stack(
        [
            jnp.exp(-decay_rates),
            residues * jnp.sqrt(-jnp.expm1(-2.0 * decay_rates)),
            jnp.exp(-decay_rates * (rows // SUBS)),
            jnp.exp(-decay_rates * rows),
        ]
    )


def spread(coef_ref, which, lanes):
    table = coef_ref[which, :, lanes]
    return [jnp.broadcast_to(table[r : r + 1, :], (SUBS, LANES)) for r in range(MODES)]


def end_states(signal_ref, lanes, decay, run, backward):
    def step(j, state):
        at = run - 1 - j if backward else j
        row = signal_ref[pl.ds(at, SUBS, stride=run), lanes]
        return tuple(a * s + row for a, s in zip(decay, state))

    zero = jnp.zeros((SUBS, LANES), jnp.float32)
    return lax.fori_loop(0, run, step, (zero,) * MODES, unroll=8)


def full_scan(signal_ref, out_ref, decay, gain, state, run, backward):
    def step(j, state):
        at = run - 1 - j if backward else j
        rows = pl.ds(at, SUBS, stride=run)
        row = signal_ref[rows, :]
        state = tuple(a * s + row for a, s in zip(decay, state))
        terms = [g * s for g, s in zip(gain, state)]
        while len(terms) > 1:
            terms = [terms[i] + terms[i + 1] for i in range(0, len(terms), 2)]
        out_ref[rows, :] = terms[0]
        return state

    lax.fori_loop(0, run, step, tuple(state), unroll=8)


def bring(sources, targets, sems):
    copies = [pltpu.make_async_copy(a, b, sems.at[i]) for i, (a, b) in enumerate(zip(sources, targets))]
    for copy in copies:
        copy.start()
    return copies


def product(order_ref, x_ref, pieces, halves, x, w, x_sems, w_sems):
    depth = x.shape[2]
    width = w.shape[2] // 3
    loads, at = [], 0
    for r, parts in enumerate(halves):
        columns = pl.ds(pl.multiple_of(order_ref[r] * depth, depth), depth)
        load = bring([x_ref.at[:, columns]], [x.at[r]], x_sems.at[pl.ds(r, 1)])
        part = depth // parts
        for i in range(parts):
            targets = [w.at[r, pl.ds(i * part, part), pl.ds(b * width, width)] for b in range(3)]
            load += bring([pieces[at].at[b] for b in range(3)], targets, w_sems.at[at])
            at += 1
        loads.append(load)
    total = None
    for r in range(len(halves)):
        for copy in loads[r]:
            copy.wait()
        term = jnp.dot(x[r], w[r], preferred_element_type=jnp.float32)
        total = term if total is None else total + term
    return total


def project_part_kernel(halves, order_ref, x_ref, *refs):
    count = sum(halves)
    pieces, (out_ref, x, w, x_sems, w_sems) = refs[:count], refs[count:]
    out_ref[...] = product(order_ref, x_ref, pieces, halves, x, w, x_sems, w_sems)


def project_kernel(run, halves, order_ref, x_ref, *refs):
    count = sum(halves)
    pieces, refs = refs[:count], refs[count:]
    part_ref, g_ref, coef_ref, proj_ref, runs_ref, ends_ref, x, w, mix, gmix, x_sems, w_sems = refs
    width = g_ref.shape[1]
    total = part_ref[...] + product(order_ref, x_ref, pieces, halves, x, w, x_sems, w_sems)
    for b in range(3):
        proj_ref[b] = total[:, b * width : (b + 1) * width].astype(jnp.bfloat16)
    for lane in range(0, width, LANES):
        lanes = slice(lane, lane + LANES)
        mix[...] = proj_ref[1, :, lanes].astype(jnp.float32) * proj_ref[2, :, lanes].astype(jnp.float32)
        gmix[...] = g_ref[:, lanes].astype(jnp.float32) * proj_ref[0, :, lanes].astype(jnp.float32)
        decay = spread(coef_ref, 0, lanes)
        long = coef_ref[2, :, lanes]
        for way, signal in enumerate((mix, gmix)):
            state = end_states(signal, slice(None), decay, run, way == 1)
            for r in range(MODES):
                runs_ref[way, lane // LANES, pl.ds(r, SUBS, stride=MODES), :] = state[r]
            total = jnp.zeros((MODES, LANES), jnp.float32)
            for i in range(SUBS):
                at = SUBS - 1 - i if way else i
                total = long * total + runs_ref[way, lane // LANES, at * MODES : (at + 1) * MODES, :]
            ends_ref[way, :, lanes] = total


def scan_kernel(run, place_ref, proj_ref, g_ref, coef_ref, skip_ref, runs_ref, ends_ref, gated_ref, gp_ref, mix, out, start):
    me = place_ref[0]
    count = ends_ref.shape[0]
    width = g_ref.shape[1]
    for lane in range(0, width, LANES):
        lanes = slice(lane, lane + LANES)
        decay = spread(coef_ref, 0, lanes)
        gain = spread(coef_ref, 1, lanes)
        long = coef_ref[2, :, lanes]
        whole = coef_ref[3, :, lanes]
        skip = skip_ref[:, lanes]
        grad = g_ref[:, lanes].astype(jnp.float32)
        query, key, value = [proj_ref[b, :, lanes].astype(jnp.float32) for b in range(3)]
        for way in range(2):
            state = jnp.zeros((MODES, LANES), jnp.float32)
            for i in range(count - 1):
                at = count - 1 - i if way else i
                keep = me < at if way else at < me
                state = jnp.where(keep, whole * state + ends_ref[at, way, :, lanes], state)
            for i in range(SUBS):
                at = SUBS - 1 - i if way else i
                start[at * MODES : (at + 1) * MODES, :] = state
                state = long * state + runs_ref[way, lane // LANES, at * MODES : (at + 1) * MODES, :]
            first = [start[pl.ds(r, SUBS, stride=MODES), :] for r in range(MODES)]
            mix[...] = grad * query if way else key * value
            full_scan(mix, out, decay, gain, first, run, way == 1)
            filtered = out[...] + skip * mix[...]
            if way:
                gp_ref[:, width + lane : width + lane + LANES] = (filtered * value).astype(jnp.bfloat16)
                gp_ref[:, 2 * width + lane : 2 * width + lane + LANES] = (filtered * key).astype(jnp.bfloat16)
            else:
                gated_ref[:, lanes] = (query * filtered).astype(jnp.bfloat16)
                gp_ref[:, lane : lane + LANES] = (grad * filtered).astype(jnp.bfloat16)


def at_rest(shape):
    return pl.BlockSpec(shape, lambda *_: (0,) * len(shape))


def away():
    return pl.BlockSpec(memory_space=pltpu.HBM)


def block_scratch(tokens, pieces, width):
    rows, inputs = tokens.shape
    depth = inputs // BLOCKS
    parts = [len(piece) for piece in pieces]
    buffers = [
        pltpu.VMEM((len(pieces), rows, depth), tokens.dtype),
        pltpu.VMEM((len(pieces), depth, 3 * width), tokens.dtype),
    ]
    return parts, buffers, [pltpu.SemaphoreType.DMA((len(pieces),)), pltpu.SemaphoreType.DMA((sum(parts), 3))]


def product_cost(tokens, pieces, width):
    rows = tokens.shape[0]
    depth = tokens.shape[1] // BLOCKS * len(pieces)
    return pl.CostEstimate(
        flops=2 * rows * depth * 3 * width, bytes_accessed=2 * depth * (rows + 3 * width), transcendentals=0
    )


def project_part(order, tokens, pieces):
    rows = tokens.shape[0]
    flat = [part for piece in pieces for part in piece]
    width = flat[0].shape[2]
    halves, buffers, sems = block_scratch(tokens, pieces, width)
    return pl.pallas_call(
        functools.partial(project_part_kernel, halves),
        grid_spec=pltpu.PrefetchScalarGridSpec(
            num_scalar_prefetch=1,
            grid=(1,),
            in_specs=[away()] * (1 + len(flat)),
            out_specs=at_rest((rows, 3 * width)),
            scratch_shapes=buffers + sems,
        ),
        out_shape=jax.ShapeDtypeStruct((rows, 3 * width), jnp.float32),
        compiler_params=pltpu.CompilerParams(vmem_limit_bytes=48 * 1024 * 1024),
        cost_estimate=product_cost(tokens, pieces, width),
        name="project_part",
    )(order, tokens, *flat)


def project(order, tokens, pieces, part, grad_out, coef):
    rows = tokens.shape[0]
    width = grad_out.shape[1]
    flat = [part for piece in pieces for part in piece]
    groups = width // LANES
    halves, buffers, sems = block_scratch(tokens, pieces, width)
    return pl.pallas_call(
        functools.partial(project_kernel, rows // SUBS, halves),
        grid_spec=pltpu.PrefetchScalarGridSpec(
            num_scalar_prefetch=1,
            grid=(1,),
            in_specs=[away()] * (1 + len(flat)) + [at_rest(a.shape) for a in (part, grad_out, coef)],
            out_specs=[
                at_rest((3, rows, width)),
                at_rest((2, groups, SUBS * MODES, LANES)),
                at_rest((2, MODES, width)),
            ],
            scratch_shapes=buffers
            + [
                pltpu.VMEM((rows, LANES), jnp.float32),
                pltpu.VMEM((rows, LANES), jnp.float32),
            ]
            + sems,
        ),
        out_shape=[
            jax.ShapeDtypeStruct((3, rows, width), jnp.bfloat16),
            jax.ShapeDtypeStruct((2, groups, SUBS * MODES, LANES), jnp.float32),
            jax.ShapeDtypeStruct((2, MODES, width), jnp.float32),
        ],
        compiler_params=pltpu.CompilerParams(vmem_limit_bytes=48 * 1024 * 1024),
        cost_estimate=product_cost(tokens, pieces, width),
        name="project",
    )(order, tokens, *flat, part, grad_out, coef)


def scan(place, proj, grad_out, coef, skip, runs, ends):
    _, rows, width = proj.shape
    return pl.pallas_call(
        functools.partial(scan_kernel, rows // SUBS),
        grid_spec=pltpu.PrefetchScalarGridSpec(
            num_scalar_prefetch=1,
            grid=(1,),
            in_specs=[at_rest(a.shape) for a in (proj, grad_out, coef, skip, runs, ends)],
            out_specs=[at_rest((rows, width)), at_rest((rows, 3 * width))],
            scratch_shapes=[
                pltpu.VMEM((rows, LANES), jnp.float32),
                pltpu.VMEM((rows, LANES), jnp.float32),
                pltpu.VMEM((SUBS * MODES, LANES), jnp.float32),
            ],
        ),
        out_shape=[
            jax.ShapeDtypeStruct((rows, width), jnp.bfloat16),
            jax.ShapeDtypeStruct((rows, 3 * width), jnp.bfloat16),
        ],
        compiler_params=pltpu.CompilerParams(vmem_limit_bytes=VMEM_BYTES // 4),
        cost_estimate=pl.CostEstimate(flops=rows * width * MODES * 16, bytes_accessed=12 * rows * width, transcendentals=0),
        name="scan",
    )(place, proj, grad_out, coef, skip, runs, ends)


def input_grad_kernel(halves, core, pick_ref, *refs):
    chunks = len(halves)
    counts = [sum(h) for h in halves]
    places, total = [], 0
    for c in range(chunks):
        width = refs[c].shape[1] // 3
        places.append([slice(total + b * width, total + (b + 1) * width) for b in range(3)])
        total += 3 * width
    grads, refs = refs[:chunks], refs[chunks:]
    pieces, refs = refs[: sum(counts)], refs[sum(counts) :]
    out_ref, weights, sems = refs
    r_wanted = pick_ref[0]
    depth = weights.shape[0]
    at = 0
    for c, parts_of in enumerate(halves):
        for r, parts in enumerate(parts_of):

            @pl.when(r_wanted == r)
            def _(c=c, r=r, parts=parts, at=at):
                part = depth // parts
                for i in range(parts):
                    for b in range(3):
                        place = weights.at[i * part : (i + 1) * part, places[c][b]]
                        pltpu.make_async_copy(pieces[at + i].at[b], place, sems.at[c, b]).start()

            at += parts
    left = jnp.concatenate([g[...] for g in grads], axis=1)
    for c in range(chunks):
        for b in range(3):
            place = weights.at[:, places[c][b]]
            pltpu.make_async_copy(place, place, sems.at[c, b]).wait()
    tile = depth // 2

    @pl.loop(0, depth // tile)
    def _(i):
        here = pl.ds(pl.multiple_of(i * tile, tile), tile)
        total = lax.dot_general(left, weights[here, :], (((1,), (1,)), ((), ())), preferred_element_type=jnp.float32)
        out_ref[:, here] = total.astype(jnp.bfloat16)


def input_grad(pick, grads, weights, core):
    rows = grads[0].shape[0]
    depth = weights[0][0][0].shape[1]
    inner = sum(g.shape[1] for g in grads)
    halves = [[len(piece) for piece in pieces] for pieces in weights]
    flat = [part for pieces in weights for piece in pieces for part in piece]
    return pl.pallas_call(
        functools.partial(input_grad_kernel, halves, core),
        grid_spec=pltpu.PrefetchScalarGridSpec(
            num_scalar_prefetch=1,
            grid=(1,),
            in_specs=[at_rest(g.shape) for g in grads] + [away()] * len(flat),
            out_specs=at_rest((rows, depth)),
            scratch_shapes=[
                pltpu.VMEM((depth, inner), jnp.bfloat16),
                pltpu.SemaphoreType.DMA((len(grads), 3)),
            ],
        ),
        out_shape=jax.ShapeDtypeStruct((rows, depth), jnp.bfloat16),
        compiler_params=pltpu.CompilerParams(vmem_limit_bytes=60 * 1024 * 1024),
        cost_estimate=pl.CostEstimate(
            flops=2 * rows * depth * inner, bytes_accessed=2 * (inner * (rows + depth) + rows * depth), transcendentals=0
        ),
        name="input_grad",
    )(pick, *grads, *flat)


def exchange(array, axis, bit):
    count = lax.axis_size(axis)
    return lax.ppermute(array, axis, [(i, i ^ bit) for i in range(count)])


def after(value, *others):
    return lax.optimization_barrier((value, *others))[0]


class Plane:
    def __init__(self, blocks):
        self.blocks = blocks
        self.held = [{} for _ in blocks]

    def own(self, c, *gate):
        mine = after(self.blocks[c], *gate) if gate else self.blocks[c]
        self.held[c][2] = [(exchange(mine, "seq", 2),)]
        self.held[c][4] = [(exchange(mine, "seq", 4),)]
        self.held[c][0] = [(mine, exchange(mine, "seq", 1))]

    def came(self, c, *places):
        return [part[0] for where in places for part in self.held[c][where]]

    def swapped(self, c, *places):
        return [part[1] for where in places for part in self.held[c][where]]

    def relay(self, c, *gate):
        far_x, far_y = self.came(c, 2, 4)
        axis = far_x.ndim - 2
        half = far_x.shape[axis] // 2
        low = lax.slice_in_dim(far_x, 0, half, axis=axis)
        high = lax.slice_in_dim(far_y, half, 2 * half, axis=axis)
        if gate:
            low, high = after((low, high), *gate)
        self.held[c][6] = [(exchange(low, "seq", 4),), (exchange(high, "seq", 2),)]

    def swap(self, c, places, *gate):
        for where in places:
            blocks = self.came(c, where)
            if gate:
                blocks = after(blocks, *gate)
            self.held[c][where] = [(part[0], exchange(block, "seq", 1)) for part, block in zip(self.held[c][where], blocks)]

    def pieces(self, c, places=(0, 2, 4, 6)):
        return [[pair[core] for pair in self.held[c][where]] for where in places for core in (0, 1)]


def gather_whole(mine):
    whole = lax.all_gather(mine, "seq", axis=1, tiled=True)
    return [[piece] for piece in jnp.split(whole, BLOCKS, axis=1)]


def local(tokens, proj_weight, residues, decay_rates, skip_gain, grad_out):
    rows = tokens.shape[0]
    depth = proj_weight.shape[0]
    channels = skip_gain.shape[0]
    groups = lax.axis_size("chan")
    me = lax.axis_index("seq").astype(jnp.int32)
    z = lax.axis_index("chan").astype(jnp.int32)
    direct = lax.axis_size("seq") == BLOCKS and groups == 4
    order = jnp.arange(BLOCKS, dtype=jnp.int32)
    if direct:
        order = order ^ me
    coef = coefficients(residues, decay_rates, rows)
    skip = skip_gain[None, :]
    branches = proj_weight.swapaxes(0, 1)
    slots, first = [], 0
    while first < channels:
        width = WIDTHS[min(len(slots), len(WIDTHS) - 1)]
        slots.append(slice(first, first + width))
        first += width
    chunks = len(slots)
    mine = [branches[:, :, lanes] for lanes in slots]

    def forward(c, pieces, part):
        lanes = slots[c]
        count = len(pieces)
        return project(order[BLOCKS - count :], tokens, pieces, part, grad_out[:, lanes], coef[:, :, lanes])

    def meet(made):
        return lax.all_gather(jnp.concatenate([m[2] for m in made], axis=2), "seq")

    def scans(span, made, seen):
        gated, grads = [], []
        start = slots[span[0]].start
        for i, c in enumerate(span):
            lanes = slots[c]
            proj, runs, _ = made[i]
            ends = seen[:, :, :, lanes.start - start : lanes.stop - start]
            gate, grad = scan(me.reshape(1), proj, grad_out[:, lanes], coef[:, :, lanes], skip[:, lanes], runs, ends)
            gated.append(gate)
            grads.append(grad)
        return gated, grads

    if not direct:
        weights = [gather_whole(a) for a in mine]
        made = []
        for c in range(chunks):
            part = project_part(order[:6], tokens, weights[c][:6])
            made.append(forward(c, weights[c][6:], part))
        gated, grads = scans(range(chunks), made, meet(made))
        flat = [jnp.concatenate([p[0][b] for p in pieces], axis=0) for pieces in weights for b in range(3)]
        contract = (((1,), (1,)), ((), ()))
        dx = lax.dot_general(jnp.concatenate(grads, axis=1), jnp.concatenate(flat, axis=1), contract, preferred_element_type=jnp.float32)
        grad_tokens = lax.psum_scatter(dx.astype(jnp.bfloat16), "chan", scatter_dimension=1, tiled=True)
        return (jnp.concatenate(gated, axis=1), grad_tokens)

    plane = Plane(mine)
    near, far = (0, 2, 4), (6,)
    plane.own(0)
    plane.relay(0)
    plane.swap(0, (2, 4))
    plane.own(1, *plane.swapped(0, 0, 2, 4))
    plane.swap(0, far)
    part = project_part(order[:6], tokens, plane.pieces(0, near))
    made = [forward(0, plane.pieces(0, far), part)]
    seen = meet(made)
    plane.relay(1, seen)
    plane.swap(1, (2, 4), seen)
    gated, grads = scans((0,), made, seen)
    part = project_part(order[:6], tokens, plane.pieces(1, near))
    plane.swap(1, far, part, grads[0])
    made.append(forward(1, plane.pieces(1, far), part))
    late = scans((1,), made[1:], meet(made[1:]))
    gated, grads = gated + late[0], grads + late[1]
    weights = [plane.pieces(c) for c in range(chunks)]

    turns = jnp.array([[3, 2, 1, 0], [3, 2, 0, 1], [0, 1, 3, 2], [0, 1, 2, 3]], jnp.int32)[z]
    inwards, across, outwards = [(0, 1), (3, 2)], [(1, 2), (2, 1)], [(1, 0), (2, 3)]

    def part(turn, core):
        pick = me ^ (2 * turns[turn] + core)
        return input_grad(pick.reshape(1), grads, weights, core)

    def add(*terms):
        return sum(t.astype(jnp.float32) for t in terms).astype(jnp.bfloat16)

    sent = []

    def send(block, pairs):
        return lax.ppermute(block, "chan", pairs)

    parts = [[None, None] for _ in range(4)]
    got = [[None, None] for _ in range(3)]
    swapped = [[None, None] for _ in range(3)]
    for turn in range(3):
        for core in range(2):
            parts[turn][core] = part(turn, core)
            block = parts[turn][core]
            if len(sent) >= 2:
                block = after(block, sent[-2])
            got[turn][core] = send(block, inwards)
            sent.append(got[turn][core])
            if turn:
                swapped[turn][core] = send(add(parts[turn - 1][core], got[turn - 1][core]), across)
    out = []
    for core in range(2):
        last = part(3, core)
        back = send(add(parts[2][core], swapped[1][core]), outwards)
        out.append(add(last, got[2][core], swapped[2][core], back))
    return (jnp.concatenate(gated, axis=1), jnp.concatenate(out, axis=1))


def solution(mesh):
    placed = (
        P("seq", None),
        P("seq", None, "chan"),
        P(None, "chan"),
        P(None, "chan"),
        P("chan"),
        P("seq", "chan"),
    )
    return jax.shard_map(
        local,
        mesh=mesh,
        in_specs=placed,
        out_specs=(P("seq", "chan"), P("seq", "chan")),
        check_vma=False,
    )
```

profile of v0, /device:TPU:0, one launch (start us, length us, event | category | flops | bytes accessed | tf_op | source)
XLA Modules:
  0.0 302.3 jit_solution(15851875556866546032)
XLA Ops:
  0.6 2.1 fusion
  2.8 3.0 collective-permute-start
  5.8 1.5 collective-permute-start.2
  7.3 33.0 %collective-permute-done.refs_2_.refs_4_ = bf16[3,1024,256]{2,1,0:T(8,128)(2,1)} collective-permute-done((bf16[3,1024,256]{2,1,0:T(8,128)(2,1)S(1)}, bf16[3,1024,256]{2,1,0:T(8,128)(2,1)}, u32[]{:S(2)}, u32[]{:S(2)}) %collective-permute-start) | collective-permute-done | bytes 1572896 | tf_op jit(solution)/shard_map/ppermute | solution.py:331
  40.3 1.5 collective-permute-done.2.refs_4_.refs_6_
  41.7 2.1 slice.87
  43.8 1.5 collective-permute-start.1
  45.3 2.1 slice.88
  47.4 0.8 collective-permute-start.3
  48.2 1.3 collective-permute-start.9
  50.1 14.3 %collective-permute-done.1.refs_0_.refs_8_ = bf16[3,512,256]{2,1,0:T(8,128)(2,1)} collective-permute-done((bf16[3,512,256]{2,1,0:T(8,128)(2,1)}, bf16[3,512,256]{2,1,0:T(8,128)(2,1)}, u32[]{:S(2)}, u32[]{:S(2)}) %collective-permute-start.1) | collective-permute-done | bytes 786464 | tf_op jit(solution)/shard_map/ppermute | solution.py:331
  64.5 3.6 %collective-permute-done.3.refs_1_.refs_9_ = bf16[3,512,256]{2,1,0:T(8,128)(2,1)} collective-permute-done((bf16[3,512,256]{2,1,0:T(8,128)(2,1)}, bf16[3,512,256]{2,1,0:T(8,128)(2,1)}, u32[]{:S(2)}, u32[]{:S(2)}) %collective-permute-start.3) | collective-permute-done | bytes 786464 | tf_op jit(solution)/shard_map/ppermute | solution.py:331
  68.2 1.1 fusion.1
  69.8 11.2 %project_part.2.refs_4_ = f32[512,768]{1,0:T(8,128)S(1)} custom-call(s32[6]{0:T(128)S(1)} %bitcast.28, bf16[512,8192]{1,0:T(8,128)(2,1)} %x_ref.7, bf16[3,1024,256]{2,1,0:T(8,128)(2,1)S(1)} %get-tuple-element.44.refs_0_.refs_2_, bf16[3,1024,256]{2,1,0:T(8,128)(2,1)} %collective-permute-done.6.refs_1_.refs_3_, ...), custom_call_target="tpu_custom_call" | custom-call | flops 4831838208 | bytes 15728640 | tf_op jit(solution)/shard_map/project_part/pallas_call | solution.py:186
  81.1 6.5 %project.2 = (bf16[3,512,256]{2,1,0:T(8,128)(2,1)S(1)}, f32[2,2,128,128]{3,2,1,0:T(8,128)S(1)}, f32[2,16,256]{2,1,0:T(8,128)S(1)}) custom-call(s32[2]{0:T(128)S(1)} %slice.68.order_ref, bf16[512,8192]{1,0:T(8,128)(2,1)} %x_ref.7, bf16[3,512,256]{2,1,0:T(8,128)(2,1)} %collective-permute-done.1.refs_0_.refs_8_, ...), custom_call_target="tpu_custom_call" | custom-call | flops 1610612736 | bytes 5242880 | tf_op jit(solution)/shard_map/project/pallas_call | solution.py:208
  87.6 17.0 %all-gather = f32[16,16,256]{2,1,0:T(8,128)S(1)} all-gather(f32[2,16,256]{2,1,0:T(8,128)S(1)} %get-tuple-element.25), channel_id=2, replica_groups=mesh['seq'=8,'chan'=4] {'seq'}, dimensions={0}, use_global_device_ids=true | all-gather | bytes 294912 | tf_op jit(solution)/shard_map/all_gather | solution.py:409
  105.2 1.2 slice.93
  106.4 1.6 collective-permute-start.11
  108.5 4.0 %scan.2 = (bf16[512,256]{1,0:T(8,128)(2,1)S(1)}, bf16[512,768]{1,0:T(8,128)(2,1)S(1)}) custom-call(s32[1]{0:T(128)} %bitcast.place_ref, bf16[3,512,256]{2,1,0:T(8,128)(2,1)S(1)} %get-tuple-element.23.proj_ref, bf16[512,256]{1,0:T(8,128)(2,1)S(1)} %get-tuple-element.47.refs_5_.g_ref, f32[4,16,256]{2,1,0:T(8,128)S(1)} %get-tuple-element.49.refs_6_.coef_ref, ...), custom_call_target="tpu_custom_call" | custom-call | flops 33554432 | bytes 1572864 | tf_op jit(solution)/shard_map/scan/pallas_call | solution.py:239
  112.5 1.2 copy-done.16
  113.7 1.3 copy-done.17
  115.0 9.7 %project_part.3.refs_4_ = f32[512,768]{1,0:T(8,128)S(1)} custom-call(s32[6]{0:T(128)S(1)} %bitcast.29, bf16[512,8192]{1,0:T(8,128)(2,1)} %x_ref.7, bf16[3,1024,256]{2,1,0:T(8,128)(2,1)S(1)} %get-tuple-element.27.refs_0_.refs_12_, bf16[3,1024,256]{2,1,0:T(8,128)(2,1)S(1)} %collective-permute-done.13.refs_1_.refs_13_, bf16[3,1024,256]{2,1,0:T(8,128)(2,1)} %copy-done.15, ...), custom_call_target="tpu_custom_call" | custom-call | flops 4831838208 | bytes 15728640 | tf_op jit(solution)/shard_map/project_part/pallas_call | solution.py:186
  124.7 1.1 copy-done.11
  126.3 1.2 collective-permute-done.12.refs_1_.refs_19_
  128.0 0.7 constant_dynamic-slice_fusion
  128.7 0.6 fusion.4
  130.0 1.0 collective-permute-done.17.refs_3_.refs_21_
  130.9 1.7 copy-done.12
  132.6 6.1 %project.3 = (bf16[3,512,256]{2,1,0:T(8,128)(2,1)S(1)}, f32[2,2,128,128]{3,2,1,0:T(8,128)S(1)}, f32[2,16,256]{2,1,0:T(8,128)S(1)}) custom-call(s32[2]{0:T(128)S(1)} %slice.68.order_ref, bf16[512,8192]{1,0:T(8,128)(2,1)} %x_ref.7, bf16[3,512,256]{2,1,0:T(8,128)(2,1)S(1)} %collective-permute-done.11.refs_0_.refs_18_, ...), custom_call_target="tpu_custom_call" | custom-call | flops 1610612736 | bytes 5242880 | tf_op jit(solution)/shard_map/project/pallas_call | solution.py:208
  138.8 8.6 %all-gather.1 = f32[16,16,256]{2,1,0:T(8,128)S(1)} all-gather(f32[2,16,256]{2,1,0:T(8,128)S(1)} %get-tuple-element.37), channel_id=3, replica_groups=mesh['seq'=8,'chan'=4] {'seq'}, dimensions={0}, use_global_device_ids=true | all-gather | bytes 294912 | tf_op jit(solution)/shard_map/all_gather | solution.py:409
  147.3 4.0 %scan.3 = (bf16[512,256]{1,0:T(8,128)(2,1)S(1)}, bf16[512,768]{1,0:T(8,128)(2,1)S(1)}) custom-call(s32[1]{0:T(128)} %bitcast.place_ref, bf16[3,512,256]{2,1,0:T(8,128)(2,1)S(1)} %get-tuple-element.35.proj_ref, bf16[512,256]{1,0:T(8,128)(2,1)S(1)} %get-tuple-element.46.refs_5_.g_ref, f32[4,16,256]{2,1,0:T(8,128)S(1)} %get-tuple-element.48.refs_6_.coef_ref, ...), custom_call_target="tpu_custom_call" | custom-call | flops 33554432 | bytes 1572864 | tf_op jit(solution)/shard_map/scan/pallas_call | solution.py:239
  151.3 0.9 copy-done.10
  152.2 6.3 %input_grad.15 = bf16[512,1024]{1,0:T(8,128)(2,1)} custom-call(s32[1]{0:T(128)} %bitcast.20.pick_ref, bf16[512,768]{1,0:T(8,128)(2,1)} %copy-done.9, bf16[512,768]{1,0:T(8,128)(2,1)} %copy-done.10, bf16[3,1024,256]{2,1,0:T(8,128)(2,1)} %copy-done, bf16[3,1024,256]{2,1,0:T(8,128)(2,1)} %collective-permute-done.6.refs_1_.refs_3_, ...), custom_call_target="tpu_custom_call" | custom-call | flops 1610612736 | bytes 5767168 | tf_op jit(solution)/shard_map/input_grad/pallas_call | solution.py:308
  158.5 3.5 %collective-permute-start.24 = (bf16[512,1024]{1,0:T(8,128)(2,1)}, bf16[512,1024]{1,0:T(8,128)(2,1)S(1)}, u32[]{:S(2)}, u32[]{:S(2)}) collective-permute-start(bf16[512,1024]{1,0:T(8,128)(2,1)} %input_grad.15), channel_id=1, source_target_pairs={{0,1},{3,2},{4,5},{7,6},{8,9},{11,10},{12,13},{15,14},{16,17},{19,... | collective-permute-start | bytes 3145736 | tf_op jit(solution)/shard_map/ppermute | solution.py:469
  162.1 6.4 %input_grad.11 = bf16[512,1024]{1,0:T(8,128)(2,1)} custom-call(s32[1]{0:T(128)} %bitcast.16.pick_ref, bf16[512,768]{1,0:T(8,128)(2,1)} %copy-done.9, bf16[512,768]{1,0:T(8,128)(2,1)} %copy-done.10, bf16[3,1024,256]{2,1,0:T(8,128)(2,1)} %copy-done, bf16[3,1024,256]{2,1,0:T(8,128)(2,1)} %collective-permute-done.6.refs_1_.refs_3_, ...), custom_call_target="tpu_custom_call" | custom-call | flops 1610612736 | bytes 5767168 | tf_op jit(solution)/shard_map/input_grad/pallas_call | solution.py:308
  168.5 2.4 collective-permute-start.18
  170.9 15.0 %collective-permute-done.24 = bf16[512,1024]{1,0:T(8,128)(2,1)S(1)} collective-permute-done((bf16[512,1024]{1,0:T(8,128)(2,1)}, bf16[512,1024]{1,0:T(8,128)(2,1)S(1)}, u32[]{:S(2)}, u32[]{:S(2)}) %collective-permute-start.24) | collective-permute-done | bytes 1048608 | tf_op jit(solution)/shard_map/ppermute | solution.py:469
  186.2 0.7 collective-permute-start.28
  188.2 6.4 %input_grad.14 = bf16[512,1024]{1,0:T(8,128)(2,1)} custom-call(s32[1]{0:T(128)} %bitcast.19.pick_ref, bf16[512,768]{1,0:T(8,128)(2,1)} %copy-done.9, bf16[512,768]{1,0:T(8,128)(2,1)} %copy-done.10, bf16[3,1024,256]{2,1,0:T(8,128)(2,1)} %copy-done, bf16[3,1024,256]{2,1,0:T(8,128)(2,1)} %collective-permute-done.6.refs_1_.refs_3_, ...), custom_call_target="tpu_custom_call" | custom-call | flops 1610612736 | bytes 5767168 | tf_op jit(solution)/shard_map/input_grad/pallas_call | solution.py:308
  194.6 8.1 %collective-permute-start.25 = (bf16[512,1024]{1,0:T(8,128)(2,1)}, bf16[512,1024]{1,0:T(8,128)(2,1)}, u32[]{:S(2)}, u32[]{:S(2)}) collective-permute-start(bf16[512,1024]{1,0:T(8,128)(2,1)} %input_grad.14), channel_id=1, source_target_pairs={{0,1},{3,2},{4,5},{7,6},{8,9},{11,10},{12,13},{15,14},{16,17},{19,... | collective-permute-start | bytes 3145736 | tf_op jit(solution)/shard_map/ppermute | solution.py:469
  202.7 5.6 %collective-permute-done.18 = bf16[512,1024]{1,0:T(8,128)(2,1)} collective-permute-done((bf16[512,1024]{1,0:T(8,128)(2,1)}, bf16[512,1024]{1,0:T(8,128)(2,1)}, u32[]{:S(2)}, u32[]{:S(2)}) %collective-permute-start.18) | collective-permute-done | bytes 1048608 | tf_op jit(solution)/shard_map/ppermute | solution.py:469
  208.3 2.6 add_convert_fusion.6
  210.9 1.7 collective-permute-start.22
  212.6 6.3 %input_grad.13 = bf16[512,1024]{1,0:T(8,128)(2,1)} custom-call(s32[1]{0:T(128)} %bitcast.18.pick_ref, bf16[512,768]{1,0:T(8,128)(2,1)} %copy-done.9, bf16[512,768]{1,0:T(8,128)(2,1)} %copy-done.10, bf16[3,1024,256]{2,1,0:T(8,128)(2,1)} %copy-done, bf16[3,1024,256]{2,1,0:T(8,128)(2,1)} %collective-permute-done.6.refs_1_.refs_3_, ...), custom_call_target="tpu_custom_call" | custom-call | flops 1610612736 | bytes 5767168 | tf_op jit(solution)/shard_map/input_grad/pallas_call | solution.py:308
  218.8 6.5 %input_grad.10 = bf16[512,1024]{1,0:T(8,128)(2,1)} custom-call(s32[1]{0:T(128)} %bitcast.14.pick_ref, bf16[512,768]{1,0:T(8,128)(2,1)} %copy-done.9, bf16[512,768]{1,0:T(8,128)(2,1)} %copy-done.10, bf16[3,1024,256]{2,1,0:T(8,128)(2,1)} %copy-done, bf16[3,1024,256]{2,1,0:T(8,128)(2,1)} %collective-permute-done.6.refs_1_.refs_3_, ...), custom_call_target="tpu_custom_call" | custom-call | flops 1610612736 | bytes 5767168 | tf_op jit(solution)/shard_map/input_grad/pallas_call | solution.py:308
  225.3 7.2 %collective-permute-start.19 = (bf16[512,1024]{1,0:T(8,128)(2,1)}, bf16[512,1024]{1,0:T(8,128)(2,1)}, u32[]{:S(2)}, u32[]{:S(2)}) collective-permute-start(bf16[512,1024]{1,0:T(8,128)(2,1)} %input_grad.10), channel_id=1, source_target_pairs={{0,1},{3,2},{4,5},{7,6},{8,9},{11,10},{12,13},{15,14},{16,17},{19,... | collective-permute-start | bytes 3145736 | tf_op jit(solution)/shard_map/ppermute | solution.py:469
  232.6 1.4 add_convert_fusion.1
  234.0 1.3 collective-permute-start.29
  235.3 6.4 %input_grad.9 = bf16[512,1024]{1,0:T(8,128)(2,1)} custom-call(s32[1]{0:T(128)} %bitcast.12.pick_ref, bf16[512,768]{1,0:T(8,128)(2,1)} %copy-done.9, bf16[512,768]{1,0:T(8,128)(2,1)} %copy-done.10, bf16[3,1024,256]{2,1,0:T(8,128)(2,1)} %copy-done, bf16[3,1024,256]{2,1,0:T(8,128)(2,1)} %collective-permute-done.6.refs_1_.refs_3_, ...), custom_call_target="tpu_custom_call" | custom-call | flops 1610612736 | bytes 5767168 | tf_op jit(solution)/shard_map/input_grad/pallas_call | solution.py:308
  241.7 2.7 add_convert_fusion.3
  244.5 1.8 collective-permute-start.27
  246.2 7.1 %collective-permute-start.26 = (bf16[512,1024]{1,0:T(8,128)(2,1)S(1)}, bf16[512,1024]{1,0:T(8,128)(2,1)}, u32[]{:S(2)}, u32[]{:S(2)}) collective-permute-start(bf16[512,1024]{1,0:T(8,128)(2,1)S(1)} %copy-done.18), channel_id=1, source_target_pairs={{0,1},{3,2},{4,5},{7,6},{8,9},{11,10},{12,13},{15,14},{16,17},{19,... | collective-permute-start | bytes 3145736 | tf_op jit(solution)/shard_map/ppermute | solution.py:469
  253.4 2.6 add_convert_fusion.5
  256.0 1.4 collective-permute-start.23
  257.4 2.6 add_convert_fusion.7
  260.1 1.7 collective-permute-start.21
  261.8 8.3 %collective-permute-start.20 = (bf16[512,1024]{1,0:T(8,128)(2,1)S(1)}, bf16[512,1024]{1,0:T(8,128)(2,1)}, u32[]{:S(2)}, u32[]{:S(2)}) collective-permute-start(bf16[512,1024]{1,0:T(8,128)(2,1)S(1)} %copy-done.19), channel_id=1, source_target_pairs={{0,1},{3,2},{4,5},{7,6},{8,9},{11,10},{12,13},{15,14},{16,17},{19,... | collective-permute-start | bytes 3145736 | tf_op jit(solution)/shard_map/ppermute | solution.py:469
  270.7 0.8 pad_maximum_fusion.1
  271.6 6.3 %input_grad.12 = bf16[512,1024]{1,0:T(8,128)(2,1)} custom-call(s32[1]{0:T(128)} %bitcast.17.pick_ref, bf16[512,768]{1,0:T(8,128)(2,1)} %copy-done.9, bf16[512,768]{1,0:T(8,128)(2,1)} %copy-done.10, bf16[3,1024,256]{2,1,0:T(8,128)(2,1)} %copy-done, bf16[3,1024,256]{2,1,0:T(8,128)(2,1)} %collective-permute-done.6.refs_1_.refs_3_, ...), custom_call_target="tpu_custom_call" | custom-call | flops 1610612736 | bytes 5767168 | tf_op jit(solution)/shard_map/input_grad/pallas_call | solution.py:308
  277.9 6.4 %input_grad.8 = bf16[512,1024]{1,0:T(8,128)(2,1)} custom-call(s32[1]{0:T(128)} %bitcast.10.pick_ref, bf16[512,768]{1,0:T(8,128)(2,1)} %copy-done.9, bf16[512,768]{1,0:T(8,128)(2,1)} %copy-done.10, bf16[3,1024,256]{2,1,0:T(8,128)(2,1)} %copy-done, bf16[3,1024,256]{2,1,0:T(8,128)(2,1)} %collective-permute-done.6.refs_1_.refs_3_, ...), custom_call_target="tpu_custom_call" | custom-call | flops 1610612736 | bytes 5767168 | tf_op jit(solution)/shard_map/input_grad/pallas_call | solution.py:308
  284.4 2.8 add_convert_fusion
  287.2 10.8 %collective-permute-done.20 = bf16[512,1024]{1,0:T(8,128)(2,1)} collective-permute-done((bf16[512,1024]{1,0:T(8,128)(2,1)S(1)}, bf16[512,1024]{1,0:T(8,128)(2,1)}, u32[]{:S(2)}, u32[]{:S(2)}) %collective-permute-start.20) | collective-permute-done | bytes 1048608 | tf_op jit(solution)/shard_map/ppermute | solution.py:469
  298.0 2.8 add_convert_fusion.4
  300.8 1.5 pad_maximum_fusion
  (94 shorter events, 3.9 us)
Async XLA Ops:
  2.7 67.1 %copy-start = (bf16[3,1024,256]{2,1,0:T(8,128)(2,1)}, bf16[3,1024,256]{2,1,0:T(8,128)(2,1)S(1)}, u32[]{:S(2)}) copy-start(bf16[3,1024,256]{2,1,0:T(8,128)(2,1)S(1)} %get-tuple-element.44.refs_0_.refs_2_) | copy-start | bytes 4718596
  2.7 109.8 %copy-start.1 = (bf16[3,1024,256]{2,1,0:T(8,128)(2,1)}, bf16[3,1024,256]{2,1,0:T(8,128)(2,1)S(1)}, u32[]{:S(2)}) copy-start(bf16[3,1024,256]{2,1,0:T(8,128)(2,1)S(1)} %get-tuple-element.27.refs_0_.refs_12_) | copy-start | bytes 4718596
  2.7 47.3 %copy-start.26 = (f32[16,512]{1,0:T(8,128)S(1)}, f32[16,512]{1,0:T(8,128)}, u32[]{:S(2)}) copy-start(f32[16,512]{1,0:T(8,128)} %param.10) | copy-start | bytes 98308
  2.8 47.3 %copy-start.27 = (f32[16,512]{1,0:T(8,128)S(1)}, f32[16,512]{1,0:T(8,128)}, u32[]{:S(2)}) copy-start(f32[16,512]{1,0:T(8,128)} %param.9) | copy-start | bytes 98308
  2.8 37.5 %collective-permute-start = (bf16[3,1024,256]{2,1,0:T(8,128)(2,1)S(1)}, bf16[3,1024,256]{2,1,0:T(8,128)(2,1)}, u32[]{:S(2)}, u32[]{:S(2)}) collective-permute-start(bf16[3,1024,256]{2,1,0:T(8,128)(2,1)S(1)} %get-tuple-element.44.refs_0_.refs_2_), channel_id=1, source_target_pairs={{0,8},{4,12},{8,0},{12,4},{16,24},{20,28},{24,16},{28,20},{1,9},{5... | collective-permute-start | bytes 4718600 | tf_op jit(solution)/shard_map/ppermute | solution.py:331
  5.8 36.0 %collective-permute-start.2 = (bf16[3,1024,256]{2,1,0:T(8,128)(2,1)S(1)}, bf16[3,1024,256]{2,1,0:T(8,128)(2,1)}, u32[]{:S(2)}, u32[]{:S(2)}) collective-permute-start(bf16[3,1024,256]{2,1,0:T(8,128)(2,1)S(1)} %get-tuple-element.44.refs_0_.refs_2_), channel_id=1, source_target_pairs={{0,16},{4,20},{8,24},{12,28},{16,0},{20,4},{24,8},{28,12},{1,17},{... | collective-permute-start | bytes 4718600 | tf_op jit(solution)/shard_map/ppermute | solution.py:331
  7.3 40.9 %collective-permute-start.6 = (bf16[3,1024,256]{2,1,0:T(8,128)(2,1)S(1)}, bf16[3,1024,256]{2,1,0:T(8,128)(2,1)}, u32[]{:S(2)}, u32[]{:S(2)}) collective-permute-start(bf16[3,1024,256]{2,1,0:T(8,128)(2,1)S(1)} %get-tuple-element.44.refs_0_.refs_2_), channel_id=1, source_target_pairs={{0,4},{4,0},{8,12},{12,8},{16,20},{20,16},{24,28},{28,24},{1,5},{5... | collective-permute-start | bytes 4718600 | tf_op jit(solution)/shard_map/ppermute | solution.py:331
  40.3 7.9 %collective-permute-start.7 = (bf16[3,1024,256]{2,1,0:T(8,128)(2,1)}, bf16[3,1024,256]{2,1,0:T(8,128)(2,1)}, u32[]{:S(2)}, u32[]{:S(2)}) collective-permute-start(bf16[3,1024,256]{2,1,0:T(8,128)(2,1)} %collective-permute-done.refs_2_.refs_4_), channel_id=1, source_target_pairs={{0,4},{4,0},{8,12},{12,8},{16,20},{20,16},{24,28},{28,24},{1,5},{5... | collective-permute-start | bytes 4718600 | tf_op jit(solution)/shard_map/ppermute | solution.py:331
  41.7 6.5 %collective-permute-start.8 = (bf16[3,1024,256]{2,1,0:T(8,128)(2,1)}, bf16[3,1024,256]{2,1,0:T(8,128)(2,1)}, u32[]{:S(2)}, u32[]{:S(2)}) collective-permute-start(bf16[3,1024,256]{2,1,0:T(8,128)(2,1)} %collective-permute-done.2.refs_4_.refs_6_), channel_id=1, source_target_pairs={{0,4},{4,0},{8,12},{12,8},{16,20},{20,16},{24,28},{28,24},{1,5},{5... | collective-permute-start | bytes 4718600 | tf_op jit(solution)/shard_map/ppermute | solution.py:331
  43.8 20.7 %collective-permute-start.1 = (bf16[3,512,256]{2,1,0:T(8,128)(2,1)}, bf16[3,512,256]{2,1,0:T(8,128)(2,1)}, u32[]{:S(2)}, u32[]{:S(2)}) collective-permute-start(bf16[3,512,256]{2,1,0:T(8,128)(2,1)} %slice.87), channel_id=1, source_target_pairs={{0,16},{4,20},{8,24},{12,28},{16,0},{20,4},{24,8},{28,12},{1,17},{... | collective-permute-start | bytes 2359304 | tf_op jit(solution)/shard_map/ppermute | solution.py:331
  47.4 20.7 %collective-permute-start.3 = (bf16[3,512,256]{2,1,0:T(8,128)(2,1)}, bf16[3,512,256]{2,1,0:T(8,128)(2,1)}, u32[]{:S(2)}, u32[]{:S(2)}) collective-permute-start(bf16[3,512,256]{2,1,0:T(8,128)(2,1)} %slice.88), channel_id=1, source_target_pairs={{0,8},{4,12},{8,0},{12,4},{16,24},{20,28},{24,16},{28,20},{1,9},{5... | collective-permute-start | bytes 2359304 | tf_op jit(solution)/shard_map/ppermute | solution.py:331
  48.2 56.4 %collective-permute-start.9 = (bf16[3,1024,256]{2,1,0:T(8,128)(2,1)S(1)}, bf16[3,1024,256]{2,1,0:T(8,128)(2,1)S(1)}, u32[]{:S(2)}, u32[]{:S(2)}) collective-permute-start(bf16[3,1024,256]{2,1,0:T(8,128)(2,1)S(1)} %get-tuple-element.27.refs_0_.refs_12_), channel_id=1, source_target_pairs={{0,8},{4,12},{8,0},{12,4},{16,24},{20,28},{24,16},{28,20},{1,9},{5... | collective-permute-start | bytes 4718600 | tf_op jit(solution)/shard_map/ppermute | solution.py:331
  49.5 55.5 %collective-permute-start.10 = (bf16[3,1024,256]{2,1,0:T(8,128)(2,1)S(1)}, bf16[3,1024,256]{2,1,0:T(8,128)(2,1)}, u32[]{:S(2)}, u32[]{:S(2)}) collective-permute-start(bf16[3,1024,256]{2,1,0:T(8,128)(2,1)S(1)} %get-tuple-element.27.refs_0_.refs_12_), channel_id=1, source_target_pairs={{0,16},{4,20},{8,24},{12,28},{16,0},{20,4},{24,8},{28,12},{1,17},{... | collective-permute-start | bytes 4718600 | tf_op jit(solution)/shard_map/ppermute | solution.py:331
  64.4 16.6 %collective-permute-start.4 = (bf16[3,512,256]{2,1,0:T(8,128)(2,1)}, bf16[3,512,256]{2,1,0:T(8,128)(2,1)S(1)}, u32[]{:S(2)}, u32[]{:S(2)}) collective-permute-start(bf16[3,512,256]{2,1,0:T(8,128)(2,1)} %collective-permute-done.1.refs_0_.refs_8_), channel_id=1, source_target_pairs={{0,4},{4,0},{8,12},{12,8},{16,20},{20,16},{24,28},{28,24},{1,5},{5... | collective-permute-start | bytes 2359304 | tf_op jit(solution)/shard_map/ppermute | solution.py:331
  68.1 13.0 %collective-permute-start.5 = (bf16[3,512,256]{2,1,0:T(8,128)(2,1)}, bf16[3,512,256]{2,1,0:T(8,128)(2,1)S(1)}, u32[]{:S(2)}, u32[]{:S(2)}) collective-permute-start(bf16[3,512,256]{2,1,0:T(8,128)(2,1)} %collective-permute-done.3.refs_1_.refs_9_), channel_id=1, source_target_pairs={{0,4},{4,0},{8,12},{12,8},{16,20},{20,16},{24,28},{28,24},{1,5},{5... | collective-permute-start | bytes 2359304 | tf_op jit(solution)/shard_map/ppermute | solution.py:331
  69.2 43.2 %collective-permute-start.13 = (bf16[3,1024,256]{2,1,0:T(8,128)(2,1)S(1)}, bf16[3,1024,256]{2,1,0:T(8,128)(2,1)S(1)}, u32[]{:S(2)}, u32[]{:S(2)}) collective-permute-start(bf16[3,1024,256]{2,1,0:T(8,128)(2,1)S(1)} %get-tuple-element.27.refs_0_.refs_12_), channel_id=1, source_target_pairs={{0,4},{4,0},{8,12},{12,8},{16,20},{20,16},{24,28},{28,24},{1,5},{5... | collective-permute-start | bytes 4718600 | tf_op jit(solution)/shard_map/ppermute | solution.py:331
  81.1 6.5 %copy-start.3 = (bf16[3,512,256]{2,1,0:T(8,128)(2,1)}, bf16[3,512,256]{2,1,0:T(8,128)(2,1)S(1)}, u32[]{:S(2)}) copy-start(bf16[3,512,256]{2,1,0:T(8,128)(2,1)S(1)} %collective-permute-done.4.refs_2_.refs_10_) | copy-start | bytes 2359300
  81.1 6.5 %copy-start.4 = (bf16[3,512,256]{2,1,0:T(8,128)(2,1)}, bf16[3,512,256]{2,1,0:T(8,128)(2,1)S(1)}, u32[]{:S(2)}) copy-start(bf16[3,512,256]{2,1,0:T(8,128)(2,1)S(1)} %collective-permute-done.5.refs_3_.refs_11_) | copy-start | bytes 2359300
  87.6 20.8 %copy-start.28 = (f32[512]{0:T(512)S(1)}, f32[512]{0:T(512)}, u32[]{:S(2)}) copy-start(f32[512]{0:T(512)} %param.11) | copy-start | bytes 6148
  104.6 7.8 %copy-start.15 = (bf16[3,1024,256]{2,1,0:T(8,128)(2,1)}, bf16[3,1024,256]{2,1,0:T(8,128)(2,1)S(1)}, u32[]{:S(2)}) copy-start(bf16[3,1024,256]{2,1,0:T(8,128)(2,1)S(1)} %collective-permute-done.9.refs_2_.refs_14_) | copy-start | bytes 4718596
  104.6 7.9 %collective-permute-start.14 = (bf16[3,1024,256]{2,1,0:T(8,128)(2,1)S(1)}, bf16[3,1024,256]{2,1,0:T(8,128)(2,1)S(1)}, u32[]{:S(2)}, u32[]{:S(2)}) collective-permute-start(bf16[3,1024,256]{2,1,0:T(8,128)(2,1)S(1)} %collective-permute-done.9.refs_2_.refs_14_), channel_id=1, source_target_pairs={{0,4},{4,0},{8,12},{12,8},{16,20},{20,16},{24,28},{28,24},{1,5},{5... | collective-permute-start | bytes 4718600 | tf_op jit(solution)/shard_map/ppermute | solution.py:331
  105.0 7.5 %collective-permute-start.15 = (bf16[3,1024,256]{2,1,0:T(8,128)(2,1)}, bf16[3,1024,256]{2,1,0:T(8,128)(2,1)S(1)}, u32[]{:S(2)}, u32[]{:S(2)}) collective-permute-start(bf16[3,1024,256]{2,1,0:T(8,128)(2,1)} %collective-permute-done.10.refs_4_.refs_16_), channel_id=1, source_target_pairs={{0,4},{4,0},{8,12},{12,8},{16,20},{20,16},{24,28},{28,24},{1,5},{5... | collective-permute-start | bytes 4718600 | tf_op jit(solution)/shard_map/ppermute | solution.py:331
  106.4 19.9 %collective-permute-start.11 = (bf16[3,512,256]{2,1,0:T(8,128)(2,1)S(1)}, bf16[3,512,256]{2,1,0:T(8,128)(2,1)S(1)}, u32[]{:S(2)}, u32[]{:S(2)}) collective-permute-start(bf16[3,512,256]{2,1,0:T(8,128)(2,1)S(1)} %slice.92), channel_id=1, source_target_pairs={{0,16},{4,20},{8,24},{12,28},{16,0},{20,4},{24,8},{28,12},{1,17},{... | collective-permute-start | bytes 2359304 | tf_op jit(solution)/shard_map/ppermute | solution.py:331
  107.9 19.6 %collective-permute-start.12 = (bf16[3,512,256]{2,1,0:T(8,128)(2,1)S(1)}, bf16[3,512,256]{2,1,0:T(8,128)(2,1)S(1)}, u32[]{:S(2)}, u32[]{:S(2)}) collective-permute-start(bf16[3,512,256]{2,1,0:T(8,128)(2,1)S(1)} %slice.93), channel_id=1, source_target_pairs={{0,8},{4,12},{8,0},{12,4},{16,24},{20,28},{24,16},{28,20},{1,9},{5... | collective-permute-start | bytes 2359304 | tf_op jit(solution)/shard_map/ppermute | solution.py:331
  112.4 12.2 %copy-start.9 = (bf16[512,768]{1,0:T(8,128)(2,1)}, bf16[512,768]{1,0:T(8,128)(2,1)S(1)}, u32[]{:S(2)}) copy-start(bf16[512,768]{1,0:T(8,128)(2,1)S(1)} %get-tuple-element.32.refs_0_) | copy-start | bytes 2359300
  112.5 12.2 %copy-start.13 = (bf16[512,256]{1,0:T(8,128)(2,1)}, bf16[512,256]{1,0:T(8,128)(2,1)S(1)}, u32[]{:S(2)}) copy-start(bf16[512,256]{1,0:T(8,128)(2,1)S(1)} %get-tuple-element.26) | copy-start | bytes 786436
  112.5 12.2 %copy-start.2 = (bf16[3,1024,256]{2,1,0:T(8,128)(2,1)}, bf16[3,1024,256]{2,1,0:T(8,128)(2,1)S(1)}, u32[]{:S(2)}) copy-start(bf16[3,1024,256]{2,1,0:T(8,128)(2,1)S(1)} %collective-permute-done.13.refs_1_.refs_13_) | copy-start | bytes 4718596
  112.5 1.2 copy-start.16
  113.7 1.3 copy-start.17
  124.7 1.2 copy-start.11
  126.3 12.4 %copy-start.5 = (bf16[3,512,256]{2,1,0:T(8,128)(2,1)}, bf16[3,512,256]{2,1,0:T(8,128)(2,1)S(1)}, u32[]{:S(2)}) copy-start(bf16[3,512,256]{2,1,0:T(8,128)(2,1)S(1)} %collective-permute-done.11.refs_0_.refs_18_) | copy-start | bytes 2359300
  127.5 11.2 %copy-start.6 = (bf16[3,512,256]{2,1,0:T(8,128)(2,1)}, bf16[3,512,256]{2,1,0:T(8,128)(2,1)S(1)}, u32[]{:S(2)}) copy-start(bf16[3,512,256]{2,1,0:T(8,128)(2,1)S(1)} %collective-permute-done.12.refs_1_.refs_19_) | copy-start | bytes 2359300
  127.5 2.4 collective-permute-start.16
  127.5 3.4 %collective-permute-start.17 = (bf16[3,512,256]{2,1,0:T(8,128)(2,1)S(1)}, bf16[3,512,256]{2,1,0:T(8,128)(2,1)S(1)}, u32[]{:S(2)}, u32[]{:S(2)}) collective-permute-start(bf16[3,512,256]{2,1,0:T(8,128)(2,1)S(1)} %collective-permute-done.12.refs_1_.refs_19_), channel_id=1, source_target_pairs={{0,4},{4,0},{8,12},{12,8},{16,20},{20,16},{24,28},{28,24},{1,5},{5... | collective-permute-start | bytes 2359304 | tf_op jit(solution)/shard_map/ppermute | solution.py:331
  129.9 8.8 %copy-start.7 = (bf16[3,512,256]{2,1,0:T(8,128)(2,1)}, bf16[3,512,256]{2,1,0:T(8,128)(2,1)S(1)}, u32[]{:S(2)}) copy-start(bf16[3,512,256]{2,1,0:T(8,128)(2,1)S(1)} %collective-permute-done.16.refs_2_.refs_20_) | copy-start | bytes 2359300
  130.9 7.8 %copy-start.8 = (bf16[3,512,256]{2,1,0:T(8,128)(2,1)}, bf16[3,512,256]{2,1,0:T(8,128)(2,1)S(1)}, u32[]{:S(2)}) copy-start(bf16[3,512,256]{2,1,0:T(8,128)(2,1)S(1)} %collective-permute-done.17.refs_3_.refs_21_) | copy-start | bytes 2359300
  130.9 1.7 copy-start.12
  151.3 0.9 copy-start.10
  158.5 27.3 %collective-permute-start.24 = (bf16[512,1024]{1,0:T(8,128)(2,1)}, bf16[512,1024]{1,0:T(8,128)(2,1)S(1)}, u32[]{:S(2)}, u32[]{:S(2)}) collective-permute-start(bf16[512,1024]{1,0:T(8,128)(2,1)} %input_grad.15), channel_id=1, source_target_pairs={{0,1},{3,2},{4,5},{7,6},{8,9},{11,10},{12,13},{15,14},{16,17},{19,... | collective-permute-start | bytes 3145736 | tf_op jit(solution)/shard_map/ppermute | solution.py:469
  162.1 23.7 %copy-start.25 = (bf16[512,1024]{1,0:T(8,128)(2,1)S(1)}, bf16[512,1024]{1,0:T(8,128)(2,1)}, u32[]{:S(2)}) copy-start(bf16[512,1024]{1,0:T(8,128)(2,1)} %input_grad.15) | copy-start | bytes 3145732
  168.5 39.8 %collective-permute-start.18 = (bf16[512,1024]{1,0:T(8,128)(2,1)}, bf16[512,1024]{1,0:T(8,128)(2,1)}, u32[]{:S(2)}, u32[]{:S(2)}) collective-permute-start(bf16[512,1024]{1,0:T(8,128)(2,1)} %input_grad.11), channel_id=1, source_target_pairs={{0,1},{3,2},{4,5},{7,6},{8,9},{11,10},{12,13},{15,14},{16,17},{19,... | collective-permute-start | bytes 3145736 | tf_op jit(solution)/shard_map/ppermute | solution.py:469
  186.2 46.3 %collective-permute-start.28 = (bf16[512,1024]{1,0:T(8,128)(2,1)S(1)}, bf16[512,1024]{1,0:T(8,128)(2,1)S(1)}, u32[]{:S(2)}, u32[]{:S(2)}) collective-permute-start(bf16[512,1024]{1,0:T(8,128)(2,1)S(1)} %add_convert_fusion.2), channel_id=1, source_target_pairs={{1,2},{2,1},{5,6},{6,5},{9,10},{10,9},{13,14},{14,13},{17,18},{18,... | collective-permute-start | bytes 3145736 | tf_op jit(solution)/shard_map/ppermute | solution.py:469
  188.2 20.1 %copy-start.22 = (bf16[512,1024]{1,0:T(8,128)(2,1)S(1)}, bf16[512,1024]{1,0:T(8,128)(2,1)}, u32[]{:S(2)}) copy-start(bf16[512,1024]{1,0:T(8,128)(2,1)} %input_grad.11) | copy-start | bytes 3145732
  194.6 47.1 %collective-permute-start.25 = (bf16[512,1024]{1,0:T(8,128)(2,1)}, bf16[512,1024]{1,0:T(8,128)(2,1)}, u32[]{:S(2)}, u32[]{:S(2)}) collective-permute-start(bf16[512,1024]{1,0:T(8,128)(2,1)} %input_grad.14), channel_id=1, source_target_pairs={{0,1},{3,2},{4,5},{7,6},{8,9},{11,10},{12,13},{15,14},{16,17},{19,... | collective-permute-start | bytes 3145736 | tf_op jit(solution)/shard_map/ppermute | solution.py:469
  210.9 42.5 %collective-permute-start.22 = (bf16[512,1024]{1,0:T(8,128)(2,1)}, bf16[512,1024]{1,0:T(8,128)(2,1)}, u32[]{:S(2)}, u32[]{:S(2)}) collective-permute-start(bf16[512,1024]{1,0:T(8,128)(2,1)} %add_convert_fusion.6), channel_id=1, source_target_pairs={{1,2},{2,1},{5,6},{6,5},{9,10},{10,9},{13,14},{14,13},{17,18},{18,... | collective-permute-start | bytes 3145736 | tf_op jit(solution)/shard_map/ppermute | solution.py:469
  218.8 13.7 %copy-start.18 = (bf16[512,1024]{1,0:T(8,128)(2,1)S(1)}, bf16[512,1024]{1,0:T(8,128)(2,1)}, u32[]{:S(2)}) copy-start(bf16[512,1024]{1,0:T(8,128)(2,1)} %input_grad.13) | copy-start | bytes 3145732
  225.3 32.1 %collective-permute-start.19 = (bf16[512,1024]{1,0:T(8,128)(2,1)}, bf16[512,1024]{1,0:T(8,128)(2,1)}, u32[]{:S(2)}, u32[]{:S(2)}) collective-permute-start(bf16[512,1024]{1,0:T(8,128)(2,1)} %input_grad.10), channel_id=1, source_target_pairs={{0,1},{3,2},{4,5},{7,6},{8,9},{11,10},{12,13},{15,14},{16,17},{19,... | collective-permute-start | bytes 3145736 | tf_op jit(solution)/shard_map/ppermute | solution.py:469
  234.0 27.9 %collective-permute-start.29 = (bf16[512,1024]{1,0:T(8,128)(2,1)}, bf16[512,1024]{1,0:T(8,128)(2,1)}, u32[]{:S(2)}, u32[]{:S(2)}) collective-permute-start(bf16[512,1024]{1,0:T(8,128)(2,1)} %add_convert_fusion.1), channel_id=1, source_target_pairs={{1,0},{2,3},{5,4},{6,7},{9,8},{10,11},{13,12},{14,15},{17,16},{18,... | collective-permute-start | bytes 3145736 | tf_op jit(solution)/shard_map/ppermute | solution.py:469
  235.3 6.5 %copy-start.23 = (bf16[512,1024]{1,0:T(8,128)(2,1)S(1)}, bf16[512,1024]{1,0:T(8,128)(2,1)}, u32[]{:S(2)}) copy-start(bf16[512,1024]{1,0:T(8,128)(2,1)} %input_grad.14) | copy-start | bytes 3145732
  241.7 11.7 %copy-start.19 = (bf16[512,1024]{1,0:T(8,128)(2,1)S(1)}, bf16[512,1024]{1,0:T(8,128)(2,1)}, u32[]{:S(2)}) copy-start(bf16[512,1024]{1,0:T(8,128)(2,1)} %input_grad.9) | copy-start | bytes 3145732
  244.5 13.0 %copy-start.21 = (bf16[512,1024]{1,0:T(8,128)(2,1)S(1)}, bf16[512,1024]{1,0:T(8,128)(2,1)}, u32[]{:S(2)}) copy-start(bf16[512,1024]{1,0:T(8,128)(2,1)} %input_grad.10) | copy-start | bytes 3145732
  244.5 39.9 %collective-permute-start.27 = (bf16[512,1024]{1,0:T(8,128)(2,1)}, bf16[512,1024]{1,0:T(8,128)(2,1)}, u32[]{:S(2)}, u32[]{:S(2)}) collective-permute-start(bf16[512,1024]{1,0:T(8,128)(2,1)} %add_convert_fusion.3), channel_id=1, source_target_pairs={{1,2},{2,1},{5,6},{6,5},{9,10},{10,9},{13,14},{14,13},{17,18},{18,... | collective-permute-start | bytes 3145736 | tf_op jit(solution)/shard_map/ppermute | solution.py:469
  246.2 38.1 %collective-permute-start.26 = (bf16[512,1024]{1,0:T(8,128)(2,1)S(1)}, bf16[512,1024]{1,0:T(8,128)(2,1)}, u32[]{:S(2)}, u32[]{:S(2)}) collective-permute-start(bf16[512,1024]{1,0:T(8,128)(2,1)S(1)} %copy-done.18), channel_id=1, source_target_pairs={{0,1},{3,2},{4,5},{7,6},{8,9},{11,10},{12,13},{15,14},{16,17},{19,... | collective-permute-start | bytes 3145736 | tf_op jit(solution)/shard_map/ppermute | solution.py:469
  256.0 14.8 %copy-start.14 = (bf16[512,256]{1,0:T(8,128)(2,1)S(1)}, bf16[512,256]{1,0:T(8,128)(2,1)}, u32[]{:S(2)}) copy-start(bf16[512,256]{1,0:T(8,128)(2,1)} %copy-done.13) | copy-start | bytes 786436
  256.0 31.2 %collective-permute-start.23 = (bf16[512,1024]{1,0:T(8,128)(2,1)}, bf16[512,1024]{1,0:T(8,128)(2,1)}, u32[]{:S(2)}, u32[]{:S(2)}) collective-permute-start(bf16[512,1024]{1,0:T(8,128)(2,1)} %add_convert_fusion.5), channel_id=1, source_target_pairs={{1,0},{2,3},{5,4},{6,7},{9,8},{10,11},{13,12},{14,15},{17,16},{18,... | collective-permute-start | bytes 3145736 | tf_op jit(solution)/shard_map/ppermute | solution.py:469
  260.1 27.1 %collective-permute-start.21 = (bf16[512,1024]{1,0:T(8,128)(2,1)}, bf16[512,1024]{1,0:T(8,128)(2,1)}, u32[]{:S(2)}, u32[]{:S(2)}) collective-permute-start(bf16[512,1024]{1,0:T(8,128)(2,1)} %add_convert_fusion.7), channel_id=1, source_target_pairs={{1,2},{2,1},{5,6},{6,5},{9,10},{10,9},{13,14},{14,13},{17,18},{18,... | collective-permute-start | bytes 3145736 | tf_op jit(solution)/shard_map/ppermute | solution.py:469
  261.8 36.2 %collective-permute-start.20 = (bf16[512,1024]{1,0:T(8,128)(2,1)S(1)}, bf16[512,1024]{1,0:T(8,128)(2,1)}, u32[]{:S(2)}, u32[]{:S(2)}) collective-permute-start(bf16[512,1024]{1,0:T(8,128)(2,1)S(1)} %copy-done.19), channel_id=1, source_target_pairs={{0,1},{3,2},{4,5},{7,6},{8,9},{11,10},{12,13},{15,14},{16,17},{19,... | collective-permute-start | bytes 3145736 | tf_op jit(solution)/shard_map/ppermute | solution.py:469
  277.9 6.4 %copy-start.24 = (bf16[512,1024]{1,0:T(8,128)(2,1)S(1)}, bf16[512,1024]{1,0:T(8,128)(2,1)}, u32[]{:S(2)}) copy-start(bf16[512,1024]{1,0:T(8,128)(2,1)} %input_grad.12) | copy-start | bytes 3145732
  284.3 13.7 %copy-start.20 = (bf16[512,1024]{1,0:T(8,128)(2,1)S(1)}, bf16[512,1024]{1,0:T(8,128)(2,1)}, u32[]{:S(2)}) copy-start(bf16[512,1024]{1,0:T(8,128)(2,1)} %input_grad.8) | copy-start | bytes 3145732
where the time goes:
time: 303 us; the launch traced here: 302 us
  Pallas kernels  92.4 us (30%)
  waiting for transfers between devices  86.5 us (29%)
  starting transfers between devices  57.6 us (19%)
  blocking collectives  25.5 us (8%)
  other arithmetic  20.3 us (7%)
  local copies, waits for them, and re-layouts  16.3 us (5%)
  between operations  3.63 us (1%)
    ppermute x18, waiting for transfers between devices, exchange(): return lax.ppermute(array, axis, [(i, i ^ bit) for i in range(count)])  55.1 us
    pallas_call x8, Pallas kernels, input_grad(): pl.pallas_call(functools.partial(input_grad_kernel, halves, core), grid_s...  51 us
    ppermute x12, starting transfers between devices, send(): return lax.ppermute(block, 'chan', pairs)  45.2 us
    ppermute x12, waiting for transfers between devices, send(): return lax.ppermute(block, 'chan', pairs)  31.4 us
    all_gather x2, blocking collectives, meet(): return lax.all_gather(jnp.concatenate([m[2] for m in made], axis=2), 'seq')  25.5 us
    pallas_call x2, Pallas kernels, project_part(): pl.pallas_call(functools.partial(project_part_kernel, halves), grid_spec=...  20.9 us
    convert_element_type x8, other arithmetic, add(): return sum((t.astype(jnp.float32) for t in terms)).astype(jnp.bfloat16)  17.9 us
    pallas_call x2, Pallas kernels, project(): pl.pallas_call(functools.partial(project_kernel, rows // SUBS, halves), g...  12.6 us
  transfers between devices with their start and end apart: 30, of which 10 were waited for; matrix products, arithmetic and copies ran while one was open for 8% of the time, Pallas kernels for 25%

commit v1 on v0

--- a/solution.py
+++ b/solution.py
@@ -253,13 +253,13 @@
             jax.ShapeDtypeStruct((rows, width), jnp.bfloat16),
             jax.ShapeDtypeStruct((rows, 3 * width), jnp.bfloat16),
         ],
-        compiler_params=pltpu.CompilerParams(vmem_limit_bytes=VMEM_BYTES // 4),
+        compiler_params=pltpu.CompilerParams(vmem_limit_bytes=48 * 1024 * 1024),
         cost_estimate=pl.CostEstimate(flops=rows * width * MODES * 16, bytes_accessed=12 * rows * width, transcendentals=0),
         name="scan",
     )(place, proj, grad_out, coef, skip, runs, ends)
 
 
-def input_grad_kernel(halves, core, pick_ref, *refs):
+def input_grad_kernel(halves, half, pick_ref, *refs):
     chunks = len(halves)
     counts = [sum(h) for h in halves]
     places, total = [], 0
@@ -278,11 +278,16 @@
 
             @pl.when(r_wanted == r)
             def _(c=c, r=r, parts=parts, at=at):
-                part = depth // parts
-                for i in range(parts):
+                if half is None:
+                    part = depth // parts
+                    moves = [(pieces[at + i], slice(i * part, (i + 1) * part)) for i in range(parts)]
+                elif parts == 2:
+                    moves = [(pieces[at + half], slice(0, depth))]
+                else:
+                    moves = [(pieces[at].at[:, half * depth : (half + 1) * depth, :], slice(0, depth))]
+                for source, rows in moves:
                     for b in range(3):
-                        place = weights.at[i * part : (i + 1) * part, places[c][b]]
-                        pltpu.make_async_copy(pieces[at + i].at[b], place, sems.at[c, b]).start()
+                        pltpu.make_async_copy(source.at[b], weights.at[rows, places[c][b]], sems.at[c, b]).start()
 
             at += parts
     left = jnp.concatenate([g[...] for g in grads], axis=1)
@@ -299,14 +304,14 @@
         out_ref[:, here] = total.astype(jnp.bfloat16)
 
 
-def input_grad(pick, grads, weights, core):
+def input_grad(pick, grads, weights, half=None):
     rows = grads[0].shape[0]
-    depth = weights[0][0][0].shape[1]
+    depth = weights[0][0][0].shape[1] // (1 if half is None else 2)
     inner = sum(g.shape[1] for g in grads)
     halves = [[len(piece) for piece in pieces] for pieces in weights]
     flat = [part for pieces in weights for piece in pieces for part in piece]
     return pl.pallas_call(
-        functools.partial(input_grad_kernel, halves, core),
+        functools.partial(input_grad_kernel, halves, half),
         grid_spec=pltpu.PrefetchScalarGridSpec(
             num_scalar_prefetch=1,
             grid=(1,),
@@ -318,7 +323,7 @@
             ],
         ),
         out_shape=jax.ShapeDtypeStruct((rows, depth), jnp.bfloat16),
-        compiler_params=pltpu.CompilerParams(vmem_limit_bytes=60 * 1024 * 1024),
+        compiler_params=pltpu.CompilerParams(vmem_limit_bytes=(60 if half is None else 32) * 1024 * 1024),
         cost_estimate=pl.CostEstimate(
             flops=2 * rows * depth * inner, bytes_accessed=2 * (inner * (rows + depth) + rows * depth), transcendentals=0
         ),
@@ -456,9 +461,9 @@
     turns = jnp.array([[3, 2, 1, 0], [3, 2, 0, 1], [0, 1, 3, 2], [0, 1, 2, 3]], jnp.int32)[z]
     inwards, across, outwards = [(0, 1), (3, 2)], [(1, 2), (2, 1)], [(1, 0), (2, 3)]
 
-    def part(turn, core):
+    def part(turn, core, half=None):
         pick = me ^ (2 * turns[turn] + core)
-        return input_grad(pick.reshape(1), grads, weights, core)
+        return input_grad(pick.reshape(1), grads, weights, half)
 
     def add(*terms):
         return sum(t.astype(jnp.float32) for t in terms).astype(jnp.bfloat16)
@@ -473,10 +478,23 @@
     swapped = [[None, None] for _ in range(3)]
     for turn in range(3):
         for core in range(2):
+            if turn == core == 0:
+                pair = [part(0, 0, half) for half in range(2)]
+                parts[0][0] = jnp.concatenate(pair, axis=1)
+                got[0][0] = jnp.concatenate([send(block, inwards) for block in pair], axis=1)
+                sent.append(got[0][0])
+                continue
             parts[turn][core] = part(turn, core)
             block = parts[turn][core]
             if len(sent) >= 2:
                 block = after(block, sent[-2])
+            if turn == 2 and core == 1:
+                half = block.shape[1] // 2
+                first = send(block[:, :half], inwards)
+                second = send(block[:, half:], inwards)
+                got[turn][core] = (first, second)
+                swapped[turn][core] = send(add(parts[turn - 1][core], got[turn - 1][core]), across)
+                continue
             got[turn][core] = send(block, inwards)
             sent.append(got[turn][core])
             if turn:
@@ -485,7 +503,12 @@
     for core in range(2):
         last = part(3, core)
         back = send(add(parts[2][core], swapped[1][core]), outwards)
-        out.append(add(last, got[2][core], swapped[2][core], back))
+        if core:
+            rest = [last, swapped[2][core], back]
+            half = last.shape[1] // 2
+            out += [add(*[a[:, i * half : (i + 1) * half] for a in rest], got[2][core][i]) for i in range(2)]
+        else:
+            out.append(add(last, got[2][core], swapped[2][core], back))
     return (jnp.concatenate(gated, axis=1), jnp.concatenate(out, axis=1))
 
 

time: 303 us -> 299 us (0.987)
  waiting for transfers between devices: 86.5 us -> 81.7 us
    ppermute x12 -> x14, waiting for transfers between devices: 31.4 us -> 25 us  [send(): return lax.ppermute(block, 'chan', pairs)]
    ppermute x12 -> x14, starting transfers between devices: 45.2 us -> 43.3 us  [send(): return lax.ppermute(block, 'chan', pairs)]
    unnamed x58 -> x61, local copies, waits for them, and re-layouts: 6.32 us -> 4.95 us
    pallas_call x8 -> x9, Pallas kernels: 51 us -> 51.8 us  [input_grad(): pl.pallas_call(functools.partial(input_grad_kernel, halves, half), grid_s...]
  transfers between devices with their start and end apart: 30 -> 32, of which waited for: 10 -> 12; matrix products, arithmetic and copies ran while one was open for 8% -> 9% of each run, Pallas kernels for 25% -> 27%
where the time goes in v1:
time: 299 us; the launch traced here: 297 us
  Pallas kernels  94.3 us (32%)
  waiting for transfers between devices  81.7 us (27%)
  starting transfers between devices  55.6 us (19%)
  blocking collectives  25.4 us (8%)
  other arithmetic  21.9 us (7%)
  local copies, waits for them, and re-layouts  14.7 us (5%)
  between operations  3.82 us (1%)
    ppermute x18, waiting for transfers between devices, exchange(): return lax.ppermute(array, axis, [(i, i ^ bit) for i in range(count)])  56.8 us
    pallas_call x9, Pallas kernels, input_grad(): pl.pallas_call(functools.partial(input_grad_kernel, halves, half), grid_s...  51.8 us
    ppermute x14, starting transfers between devices, send(): return lax.ppermute(block, 'chan', pairs)  43.3 us
    all_gather x2, blocking collectives, meet(): return lax.all_gather(jnp.concatenate([m[2] for m in made], axis=2), 'seq')  25.4 us
    ppermute x14, waiting for transfers between devices, send(): return lax.ppermute(block, 'chan', pairs)  25 us
    pallas_call x2, Pallas kernels, project_part(): pl.pallas_call(functools.partial(project_part_kernel, halves), grid_spec=...  20.9 us
    convert_element_type x8, other arithmetic, add(): return sum((t.astype(jnp.float32) for t in terms)).astype(jnp.bfloat16)  19.4 us
    pallas_call x2, Pallas kernels, project(): pl.pallas_call(functools.partial(project_kernel, rows // SUBS, halves), g...  13.6 us
  transfers between devices with their start and end apart: 32, of which 12 were waited for; matrix products, arithmetic and copies ran while one was open for 9% of the time, Pallas kernels for 27%

profile of v1, /device:TPU:0, one launch (start us, length us, event | category | flops | bytes accessed | tf_op | source)
XLA Modules:
  0.0 297.5 jit_solution(15213536141047309766)
XLA Ops:
  0.6 2.1 fusion
  2.8 3.0 %collective-permute-start = (bf16[3,1024,256]{2,1,0:T(8,128)(2,1)S(1)}, bf16[3,1024,256]{2,1,0:T(8,128)(2,1)}, u32[]{:S(2)}, u32[]{:S(2)}) collective-permute-start(bf16[3,1024,256]{2,1,0:T(8,128)(2,1)S(1)} %get-tuple-element.46.refs_0_.refs_2_), channel_id=1, source_target_pairs={{0,8},{4,12},{8,0},{12,4},{16,24},{20,28},{24,16},{28,20},{1,9},{5... | collective-permute-start | bytes 4718600 | tf_op jit(solution)/shard_map/ppermute | solution.py:336
  5.8 1.5 collective-permute-start.2
  7.3 33.0 %collective-permute-done.refs_2_.refs_4_ = bf16[3,1024,256]{2,1,0:T(8,128)(2,1)} collective-permute-done((bf16[3,1024,256]{2,1,0:T(8,128)(2,1)S(1)}, bf16[3,1024,256]{2,1,0:T(8,128)(2,1)}, u32[]{:S(2)}, u32[]{:S(2)}) %collective-permute-start) | collective-permute-done | bytes 1572896 | tf_op jit(solution)/shard_map/ppermute | solution.py:336
  40.3 1.5 collective-permute-done.2.refs_4_.refs_6_
  41.7 2.1 slice.120
  43.8 1.5 collective-permute-start.1
  45.3 2.1 slice.121
  48.2 1.3 collective-permute-start.9
  50.1 14.3 %collective-permute-done.1.refs_0_.refs_8_ = bf16[3,512,256]{2,1,0:T(8,128)(2,1)} collective-permute-done((bf16[3,512,256]{2,1,0:T(8,128)(2,1)}, bf16[3,512,256]{2,1,0:T(8,128)(2,1)}, u32[]{:S(2)}, u32[]{:S(2)}) %collective-permute-start.1) | collective-permute-done | bytes 786464 | tf_op jit(solution)/shard_map/ppermute | solution.py:336
  64.5 3.6 %collective-permute-done.3.refs_1_.refs_9_ = bf16[3,512,256]{2,1,0:T(8,128)(2,1)} collective-permute-done((bf16[3,512,256]{2,1,0:T(8,128)(2,1)}, bf16[3,512,256]{2,1,0:T(8,128)(2,1)}, u32[]{:S(2)}, u32[]{:S(2)}) %collective-permute-start.3) | collective-permute-done | bytes 786464 | tf_op jit(solution)/shard_map/ppermute | solution.py:336
  68.2 1.1 fusion.2
  69.8 11.2 %project_part.2.refs_4_ = f32[512,768]{1,0:T(8,128)S(1)} custom-call(s32[6]{0:T(128)S(1)} %bitcast.28, bf16[512,8192]{1,0:T(8,128)(2,1)} %x_ref.7, bf16[3,1024,256]{2,1,0:T(8,128)(2,1)S(1)} %get-tuple-element.46.refs_0_.refs_2_, bf16[3,1024,256]{2,1,0:T(8,128)(2,1)} %collective-permute-done.6.refs_1_.refs_3_, ...), custom_call_target="tpu_custom_call" | custom-call | flops 4831838208 | bytes 15728640 | tf_op jit(solution)/shard_map/project_part/pallas_call | solution.py:186
  81.1 6.5 %project.2 = (bf16[3,512,256]{2,1,0:T(8,128)(2,1)S(1)}, f32[2,2,128,128]{3,2,1,0:T(8,128)S(1)}, f32[2,16,256]{2,1,0:T(8,128)S(1)}) custom-call(s32[2]{0:T(128)S(1)} %slice.93.order_ref, bf16[512,8192]{1,0:T(8,128)(2,1)} %x_ref.7, bf16[3,512,256]{2,1,0:T(8,128)(2,1)} %collective-permute-done.1.refs_0_.refs_8_, ...), custom_call_target="tpu_custom_call" | custom-call | flops 1610612736 | bytes 5242880 | tf_op jit(solution)/shard_map/project/pallas_call | solution.py:208
  87.6 17.0 %all-gather = f32[16,16,256]{2,1,0:T(8,128)S(1)} all-gather(f32[2,16,256]{2,1,0:T(8,128)S(1)} %get-tuple-element.25), channel_id=2, replica_groups=mesh['seq'=8,'chan'=4] {'seq'}, dimensions={0}, use_global_device_ids=true | all-gather | bytes 294912 | tf_op jit(solution)/shard_map/all_gather | solution.py:414
  105.2 1.6 collective-permute-start.11
  107.3 4.0 %scan.2 = (bf16[512,256]{1,0:T(8,128)(2,1)S(1)}, bf16[512,768]{1,0:T(8,128)(2,1)S(1)}) custom-call(s32[1]{0:T(128)} %bitcast.place_ref, bf16[3,512,256]{2,1,0:T(8,128)(2,1)S(1)} %get-tuple-element.23.proj_ref, bf16[512,256]{1,0:T(8,128)(2,1)S(1)} %get-tuple-element.51.refs_5_.g_ref, f32[4,16,256]{2,1,0:T(8,128)S(1)} %get-tuple-element.53.refs_6_.coef_ref, ...), custom_call_target="tpu_custom_call" | custom-call | flops 33554432 | bytes 1572864 | tf_op jit(solution)/shard_map/scan/pallas_call | solution.py:239
  111.4 1.2 copy-done.20
  112.6 9.7 %project_part.3.refs_4_ = f32[512,768]{1,0:T(8,128)S(1)} custom-call(s32[6]{0:T(128)S(1)} %bitcast.29, bf16[512,8192]{1,0:T(8,128)(2,1)} %x_ref.7, bf16[3,1024,256]{2,1,0:T(8,128)(2,1)S(1)} %get-tuple-element.27.refs_0_.refs_12_, bf16[3,1024,256]{2,1,0:T(8,128)(2,1)S(1)} %collective-permute-done.13.refs_1_.refs_13_, bf16[3,1024,256]{2,1,0:T(8,128)(2,1)} %copy-done.2, ...), custom_call_target="tpu_custom_call" | custom-call | flops 4831838208 | bytes 15728640 | tf_op jit(solution)/shard_map/project_part/pallas_call | solution.py:186
  122.3 1.1 copy-done.13
  123.4 1.8 collective-permute-done.11.refs_0_.refs_18_
  125.3 1.2 collective-permute-done.12.refs_1_.refs_19_
  129.1 1.1 collective-permute-done.17.refs_3_.refs_21_
  130.3 1.4 copy-done.14
  131.7 7.1 %project.3 = (bf16[3,512,256]{2,1,0:T(8,128)(2,1)S(1)}, f32[2,2,128,128]{3,2,1,0:T(8,128)S(1)}, f32[2,16,256]{2,1,0:T(8,128)S(1)}) custom-call(s32[2]{0:T(128)S(1)} %slice.93.order_ref, bf16[512,8192]{1,0:T(8,128)(2,1)} %x_ref.7, bf16[3,512,256]{2,1,0:T(8,128)(2,1)} %collective-permute-done.11.refs_0_.refs_18_, ...), custom_call_target="tpu_custom_call" | custom-call | flops 1610612736 | bytes 5242880 | tf_op jit(solution)/shard_map/project/pallas_call | solution.py:208
  138.8 8.5 %all-gather.1 = f32[16,16,256]{2,1,0:T(8,128)S(1)} all-gather(f32[2,16,256]{2,1,0:T(8,128)S(1)} %get-tuple-element.37), channel_id=3, replica_groups=mesh['seq'=8,'chan'=4] {'seq'}, dimensions={0}, use_global_device_ids=true | all-gather | bytes 294912 | tf_op jit(solution)/shard_map/all_gather | solution.py:414
  147.3 4.0 %scan.3 = (bf16[512,256]{1,0:T(8,128)(2,1)S(1)}, bf16[512,768]{1,0:T(8,128)(2,1)S(1)}) custom-call(s32[1]{0:T(128)} %bitcast.place_ref, bf16[3,512,256]{2,1,0:T(8,128)(2,1)S(1)} %get-tuple-element.35.proj_ref, bf16[512,256]{1,0:T(8,128)(2,1)S(1)} %get-tuple-element.50.refs_5_.g_ref, f32[4,16,256]{2,1,0:T(8,128)S(1)} %get-tuple-element.52.refs_6_.coef_ref, ...), custom_call_target="tpu_custom_call" | custom-call | flops 33554432 | bytes 1572864 | tf_op jit(solution)/shard_map/scan/pallas_call | solution.py:239
  151.3 3.7 %input_grad.12 = bf16[512,512]{1,0:T(8,128)(2,1)} custom-call(s32[1]{0:T(128)} %bitcast.16.pick_ref, bf16[512,768]{1,0:T(8,128)(2,1)S(1)} %copy-done.11, bf16[512,768]{1,0:T(8,128)(2,1)S(1)} %get-tuple-element.39.refs_1_, bf16[3,1024,256]{2,1,0:T(8,128)(2,1)S(1)} %get-tuple-element.46.refs_0_.refs_2_, ...), custom_call_target="tpu_custom_call" | custom-call | flops 805306368 | bytes 3670016 | tf_op jit(solution)/shard_map/input_grad/pallas_call | solution.py:313
  155.1 4.3 %collective-permute-start.18 = (bf16[512,512]{1,0:T(8,128)(2,1)}, bf16[512,512]{1,0:T(8,128)(2,1)}, u32[]{:S(2)}, u32[]{:S(2)}) collective-permute-start(bf16[512,512]{1,0:T(8,128)(2,1)} %input_grad.12), channel_id=1, source_target_pairs={{0,1},{3,2},{4,5},{7,6},{8,9},{11,10},{12,13},{15,14},{16,17},{19,... | collective-permute-start | bytes 1572872 | tf_op jit(solution)/shard_map/ppermute | solution.py:474
  159.3 3.4 %input_grad.13 = bf16[512,512]{1,0:T(8,128)(2,1)} custom-call(s32[1]{0:T(128)} %bitcast.16.pick_ref, bf16[512,768]{1,0:T(8,128)(2,1)S(1)} %copy-done.11, bf16[512,768]{1,0:T(8,128)(2,1)S(1)} %get-tuple-element.39.refs_1_, bf16[3,1024,256]{2,1,0:T(8,128)(2,1)S(1)} %get-tuple-element.46.refs_0_.refs_2_, ...), custom_call_target="tpu_custom_call" | custom-call | flops 805306368 | bytes 3670016 | tf_op jit(solution)/shard_map/input_grad/pallas_call | solution.py:313
  162.8 1.3 collective-permute-start.19
  164.1 6.3 %input_grad.16 = bf16[512,1024]{1,0:T(8,128)(2,1)} custom-call(s32[1]{0:T(128)} %bitcast.19.pick_ref, bf16[512,768]{1,0:T(8,128)(2,1)} %copy-done.10, bf16[512,768]{1,0:T(8,128)(2,1)} %copy-done.12, bf16[3,1024,256]{2,1,0:T(8,128)(2,1)} %copy-done, bf16[3,1024,256]{2,1,0:T(8,128)(2,1)} %collective-permute-done.6.refs_1_.refs_3_, ...), custom_call_target="tpu_custom_call" | custom-call | flops 1610612736 | bytes 5767168 | tf_op jit(solution)/shard_map/input_grad/pallas_call | solution.py:313
  170.5 1.4 collective-permute-start.25
  171.8 1.1 constant_dynamic-update-slice_fusion.1
  173.0 9.4 %collective-permute-done.19 = bf16[512,512]{1,0:T(8,128)(2,1)S(1)} collective-permute-done((bf16[512,512]{1,0:T(8,128)(2,1)}, bf16[512,512]{1,0:T(8,128)(2,1)S(1)}, u32[]{:S(2)}, u32[]{:S(2)}) %collective-permute-start.19) | collective-permute-done | bytes 524320 | tf_op jit(solution)/shard_map/ppermute | solution.py:474
  182.4 1.6 add_convert_fusion.5
  184.0 1.6 collective-permute-start.23
  186.2 6.4 %input_grad.11 = bf16[512,1024]{1,0:T(8,128)(2,1)} custom-call(s32[1]{0:T(128)} %bitcast.14.pick_ref, bf16[512,768]{1,0:T(8,128)(2,1)} %copy-done.10, bf16[512,768]{1,0:T(8,128)(2,1)} %copy-done.12, bf16[3,1024,256]{2,1,0:T(8,128)(2,1)} %copy-done, bf16[3,1024,256]{2,1,0:T(8,128)(2,1)} %collective-permute-done.6.refs_1_.refs_3_, ...), custom_call_target="tpu_custom_call" | custom-call | flops 1610612736 | bytes 5767168 | tf_op jit(solution)/shard_map/input_grad/pallas_call | solution.py:313
  192.7 5.6 %collective-permute-start.20 = (bf16[512,1024]{1,0:T(8,128)(2,1)}, bf16[512,1024]{1,0:T(8,128)(2,1)}, u32[]{:S(2)}, u32[]{:S(2)}) collective-permute-start(bf16[512,1024]{1,0:T(8,128)(2,1)} %input_grad.11), channel_id=1, source_target_pairs={{0,1},{3,2},{4,5},{7,6},{8,9},{11,10},{12,13},{15,14},{16,17},{19,... | collective-permute-start | bytes 3145736 | tf_op jit(solution)/shard_map/ppermute | solution.py:474
  199.5 5.3 %collective-permute-done.25 = bf16[512,1024]{1,0:T(8,128)(2,1)S(1)} collective-permute-done((bf16[512,1024]{1,0:T(8,128)(2,1)}, bf16[512,1024]{1,0:T(8,128)(2,1)S(1)}, u32[]{:S(2)}, u32[]{:S(2)}) %collective-permute-start.25) | collective-permute-done | bytes 1048608 | tf_op jit(solution)/shard_map/ppermute | solution.py:474
  204.9 1.4 add_convert_fusion.1
  206.3 1.7 collective-permute-start.28
  207.9 6.4 %input_grad.15 = bf16[512,1024]{1,0:T(8,128)(2,1)} custom-call(s32[1]{0:T(128)} %bitcast.18.pick_ref, bf16[512,768]{1,0:T(8,128)(2,1)} %copy-done.10, bf16[512,768]{1,0:T(8,128)(2,1)} %copy-done.12, bf16[3,1024,256]{2,1,0:T(8,128)(2,1)} %copy-done, bf16[3,1024,256]{2,1,0:T(8,128)(2,1)} %collective-permute-done.6.refs_1_.refs_3_, ...), custom_call_target="tpu_custom_call" | custom-call | flops 1610612736 | bytes 5767168 | tf_op jit(solution)/shard_map/input_grad/pallas_call | solution.py:313
  214.4 6.4 %input_grad.10 = bf16[512,1024]{1,0:T(8,128)(2,1)} custom-call(s32[1]{0:T(128)} %bitcast.12.pick_ref, bf16[512,768]{1,0:T(8,128)(2,1)} %copy-done.10, bf16[512,768]{1,0:T(8,128)(2,1)} %copy-done.12, bf16[3,1024,256]{2,1,0:T(8,128)(2,1)} %copy-done, bf16[3,1024,256]{2,1,0:T(8,128)(2,1)} %collective-permute-done.6.refs_1_.refs_3_, ...), custom_call_target="tpu_custom_call" | custom-call | flops 1610612736 | bytes 5767168 | tf_op jit(solution)/shard_map/input_grad/pallas_call | solution.py:313
  220.8 5.7 %collective-permute-start.26 = (bf16[512,1024]{1,0:T(8,128)(2,1)S(1)}, bf16[512,1024]{1,0:T(8,128)(2,1)}, u32[]{:S(2)}, u32[]{:S(2)}) collective-permute-start(bf16[512,1024]{1,0:T(8,128)(2,1)S(1)} %copy-done.26), channel_id=1, source_target_pairs={{0,1},{3,2},{4,5},{7,6},{8,9},{11,10},{12,13},{15,14},{16,17},{19,... | collective-permute-start | bytes 3145736 | tf_op jit(solution)/shard_map/ppermute | solution.py:474
  226.5 2.9 add_convert_fusion.4
  229.4 1.3 collective-permute-start.24
  230.7 2.6 add_convert_fusion.6
  233.3 1.7 collective-permute-start.22
  234.9 6.4 %input_grad.17 = bf16[512,1024]{1,0:T(8,128)(2,1)} custom-call(s32[1]{0:T(128)} %bitcast.20.pick_ref, bf16[512,768]{1,0:T(8,128)(2,1)} %copy-done.10, bf16[512,768]{1,0:T(8,128)(2,1)} %copy-done.12, bf16[3,1024,256]{2,1,0:T(8,128)(2,1)} %copy-done, bf16[3,1024,256]{2,1,0:T(8,128)(2,1)} %collective-permute-done.6.refs_1_.refs_3_, ...), custom_call_target="tpu_custom_call" | custom-call | flops 1610612736 | bytes 5767168 | tf_op jit(solution)/shard_map/input_grad/pallas_call | solution.py:313
  241.4 8.8 %collective-permute-start.21 = (bf16[512,1024]{1,0:T(8,128)(2,1)S(1)}, bf16[512,1024]{1,0:T(8,128)(2,1)}, u32[]{:S(2)}, u32[]{:S(2)}) collective-permute-start(bf16[512,1024]{1,0:T(8,128)(2,1)S(1)} %copy-done.22), channel_id=1, source_target_pairs={{0,1},{3,2},{4,5},{7,6},{8,9},{11,10},{12,13},{15,14},{16,17},{19,... | collective-permute-start | bytes 3145736 | tf_op jit(solution)/shard_map/ppermute | solution.py:474
  250.1 3.0 add_convert_fusion
  253.1 1.3 collective-permute-start.29
  254.4 2.7 add_convert_fusion.2
  257.1 1.7 collective-permute-start.27
  258.8 6.4 %input_grad.14 = bf16[512,1024]{1,0:T(8,128)(2,1)} custom-call(s32[1]{0:T(128)} %bitcast.17.pick_ref, bf16[512,768]{1,0:T(8,128)(2,1)} %copy-done.10, bf16[512,768]{1,0:T(8,128)(2,1)} %copy-done.12, bf16[3,1024,256]{2,1,0:T(8,128)(2,1)} %copy-done, bf16[3,1024,256]{2,1,0:T(8,128)(2,1)} %collective-permute-done.6.refs_1_.refs_3_, ...), custom_call_target="tpu_custom_call" | custom-call | flops 1610612736 | bytes 5767168 | tf_op jit(solution)/shard_map/input_grad/pallas_call | solution.py:313
  266.1 5.8 %collective-permute-start.30 = (bf16[512,512]{1,0:T(8,128)(2,1)}, bf16[512,512]{1,0:T(8,128)(2,1)S(1)}, u32[]{:S(2)}, u32[]{:S(2)}) collective-permute-start(bf16[512,512]{1,0:T(8,128)(2,1)} %get-tuple-element.48), channel_id=1, source_target_pairs={{0,1},{3,2},{4,5},{7,6},{8,9},{11,10},{12,13},{15,14},{16,17},{19,... | collective-permute-start | bytes 1572872 | tf_op jit(solution)/shard_map/ppermute | solution.py:474
  271.9 1.3 collective-permute-start.31
  274.1 6.3 %input_grad.9 = bf16[512,1024]{1,0:T(8,128)(2,1)} custom-call(s32[1]{0:T(128)} %bitcast.10.pick_ref, bf16[512,768]{1,0:T(8,128)(2,1)} %copy-done.10, bf16[512,768]{1,0:T(8,128)(2,1)} %copy-done.12, bf16[3,1024,256]{2,1,0:T(8,128)(2,1)} %copy-done, bf16[3,1024,256]{2,1,0:T(8,128)(2,1)} %collective-permute-done.6.refs_1_.refs_3_, ...), custom_call_target="tpu_custom_call" | custom-call | flops 1610612736 | bytes 5767168 | tf_op jit(solution)/shard_map/input_grad/pallas_call | solution.py:313
  280.4 3.2 %add_convert_fusion.3 = bf16[512,1024]{1,0:T(8,128)(2,1)S(1)} fusion(bf16[512,1024]{1,0:T(8,128)(2,1)} %collective-permute-done.24, bf16[512,1024]{1,0:T(8,128)(2,1)} %collective-permute-done.22, bf16[512,1024]{1,0:T(8,128)(2,1)} %collective-permute-done.21, bf16[512,1024]{1,0:T(8,128)(2,1)} %input_grad.9), kind=kLoop, calls=%fused_computation.4 | loop fusion | flops 4194304 | bytes 5242880 | tf_op jit(solution)/shard_map/convert_element_type | solution.py:469
  283.6 1.0 collective-permute-done.30
  284.6 9.2 %collective-permute-done.31 = bf16[512,512]{1,0:T(8,128)(2,1)S(1)} collective-permute-done((bf16[512,512]{1,0:T(8,128)(2,1)S(1)}, bf16[512,512]{1,0:T(8,128)(2,1)S(1)}, u32[]{:S(2)}, u32[]{:S(2)}) %collective-permute-start.31) | collective-permute-done | bytes 524320 | tf_op jit(solution)/shard_map/ppermute | solution.py:474
  293.8 2.1 add_convert_fusion.8
  295.9 1.6 pad_maximum_fusion
  (104 shorter events, 7.1 us)
Async XLA Ops:
  2.7 156.6 %copy-start = (bf16[3,1024,256]{2,1,0:T(8,128)(2,1)}, bf16[3,1024,256]{2,1,0:T(8,128)(2,1)S(1)}, u32[]{:S(2)}) copy-start(bf16[3,1024,256]{2,1,0:T(8,128)(2,1)S(1)} %get-tuple-element.46.refs_0_.refs_2_) | copy-start | bytes 4718596
  2.7 156.6 %copy-start.1 = (bf16[3,1024,256]{2,1,0:T(8,128)(2,1)}, bf16[3,1024,256]{2,1,0:T(8,128)(2,1)S(1)}, u32[]{:S(2)}) copy-start(bf16[3,1024,256]{2,1,0:T(8,128)(2,1)S(1)} %get-tuple-element.27.refs_0_.refs_12_) | copy-start | bytes 4718596
  2.7 47.3 %copy-start.27 = (f32[16,512]{1,0:T(8,128)S(1)}, f32[16,512]{1,0:T(8,128)}, u32[]{:S(2)}) copy-start(f32[16,512]{1,0:T(8,128)} %param.10) | copy-start | bytes 98308
  2.8 47.3 %copy-start.28 = (f32[16,512]{1,0:T(8,128)S(1)}, f32[16,512]{1,0:T(8,128)}, u32[]{:S(2)}) copy-start(f32[16,512]{1,0:T(8,128)} %param.9) | copy-start | bytes 98308
  2.8 37.5 %collective-permute-start = (bf16[3,1024,256]{2,1,0:T(8,128)(2,1)S(1)}, bf16[3,1024,256]{2,1,0:T(8,128)(2,1)}, u32[]{:S(2)}, u32[]{:S(2)}) collective-permute-start(bf16[3,1024,256]{2,1,0:T(8,128)(2,1)S(1)} %get-tuple-element.46.refs_0_.refs_2_), channel_id=1, source_target_pairs={{0,8},{4,12},{8,0},{12,4},{16,24},{20,28},{24,16},{28,20},{1,9},{5... | collective-permute-start | bytes 4718600 | tf_op jit(solution)/shard_map/ppermute | solution.py:336
  5.8 36.0 %collective-permute-start.2 = (bf16[3,1024,256]{2,1,0:T(8,128)(2,1)S(1)}, bf16[3,1024,256]{2,1,0:T(8,128)(2,1)}, u32[]{:S(2)}, u32[]{:S(2)}) collective-permute-start(bf16[3,1024,256]{2,1,0:T(8,128)(2,1)S(1)} %get-tuple-element.46.refs_0_.refs_2_), channel_id=1, source_target_pairs={{0,16},{4,20},{8,24},{12,28},{16,0},{20,4},{24,8},{28,12},{1,17},{... | collective-permute-start | bytes 4718600 | tf_op jit(solution)/shard_map/ppermute | solution.py:336
  7.3 40.9 %collective-permute-start.6 = (bf16[3,1024,256]{2,1,0:T(8,128)(2,1)S(1)}, bf16[3,1024,256]{2,1,0:T(8,128)(2,1)}, u32[]{:S(2)}, u32[]{:S(2)}) collective-permute-start(bf16[3,1024,256]{2,1,0:T(8,128)(2,1)S(1)} %get-tuple-element.46.refs_0_.refs_2_), channel_id=1, source_target_pairs={{0,4},{4,0},{8,12},{12,8},{16,20},{20,16},{24,28},{28,24},{1,5},{5... | collective-permute-start | bytes 4718600 | tf_op jit(solution)/shard_map/ppermute | solution.py:336
  40.3 7.9 %collective-permute-start.7 = (bf16[3,1024,256]{2,1,0:T(8,128)(2,1)}, bf16[3,1024,256]{2,1,0:T(8,128)(2,1)}, u32[]{:S(2)}, u32[]{:S(2)}) collective-permute-start(bf16[3,1024,256]{2,1,0:T(8,128)(2,1)} %collective-permute-done.refs_2_.refs_4_), channel_id=1, source_target_pairs={{0,4},{4,0},{8,12},{12,8},{16,20},{20,16},{24,28},{28,24},{1,5},{5... | collective-permute-start | bytes 4718600 | tf_op jit(solution)/shard_map/ppermute | solution.py:336
  41.7 6.5 %collective-permute-start.8 = (bf16[3,1024,256]{2,1,0:T(8,128)(2,1)}, bf16[3,1024,256]{2,1,0:T(8,128)(2,1)}, u32[]{:S(2)}, u32[]{:S(2)}) collective-permute-start(bf16[3,1024,256]{2,1,0:T(8,128)(2,1)} %collective-permute-done.2.refs_4_.refs_6_), channel_id=1, source_target_pairs={{0,4},{4,0},{8,12},{12,8},{16,20},{20,16},{24,28},{28,24},{1,5},{5... | collective-permute-start | bytes 4718600 | tf_op jit(solution)/shard_map/ppermute | solution.py:336
  43.8 20.7 %collective-permute-start.1 = (bf16[3,512,256]{2,1,0:T(8,128)(2,1)}, bf16[3,512,256]{2,1,0:T(8,128)(2,1)}, u32[]{:S(2)}, u32[]{:S(2)}) collective-permute-start(bf16[3,512,256]{2,1,0:T(8,128)(2,1)} %slice.120), channel_id=1, source_target_pairs={{0,16},{4,20},{8,24},{12,28},{16,0},{20,4},{24,8},{28,12},{1,17},{... | collective-permute-start | bytes 2359304 | tf_op jit(solution)/shard_map/ppermute | solution.py:336
  47.4 20.7 %collective-permute-start.3 = (bf16[3,512,256]{2,1,0:T(8,128)(2,1)}, bf16[3,512,256]{2,1,0:T(8,128)(2,1)}, u32[]{:S(2)}, u32[]{:S(2)}) collective-permute-start(bf16[3,512,256]{2,1,0:T(8,128)(2,1)} %slice.121), channel_id=1, source_target_pairs={{0,8},{4,12},{8,0},{12,4},{16,24},{20,28},{24,16},{28,20},{1,9},{5... | collective-permute-start | bytes 2359304 | tf_op jit(solution)/shard_map/ppermute | solution.py:336
  48.2 56.4 %collective-permute-start.9 = (bf16[3,1024,256]{2,1,0:T(8,128)(2,1)S(1)}, bf16[3,1024,256]{2,1,0:T(8,128)(2,1)S(1)}, u32[]{:S(2)}, u32[]{:S(2)}) collective-permute-start(bf16[3,1024,256]{2,1,0:T(8,128)(2,1)S(1)} %get-tuple-element.27.refs_0_.refs_12_), channel_id=1, source_target_pairs={{0,8},{4,12},{8,0},{12,4},{16,24},{20,28},{24,16},{28,20},{1,9},{5... | collective-permute-start | bytes 4718600 | tf_op jit(solution)/shard_map/ppermute | solution.py:336
  49.5 55.5 %collective-permute-start.10 = (bf16[3,1024,256]{2,1,0:T(8,128)(2,1)S(1)}, bf16[3,1024,256]{2,1,0:T(8,128)(2,1)S(1)}, u32[]{:S(2)}, u32[]{:S(2)}) collective-permute-start(bf16[3,1024,256]{2,1,0:T(8,128)(2,1)S(1)} %get-tuple-element.27.refs_0_.refs_12_), channel_id=1, source_target_pairs={{0,16},{4,20},{8,24},{12,28},{16,0},{20,4},{24,8},{28,12},{1,17},{... | collective-permute-start | bytes 4718600 | tf_op jit(solution)/shard_map/ppermute | solution.py:336
  64.4 16.6 %collective-permute-start.4 = (bf16[3,512,256]{2,1,0:T(8,128)(2,1)}, bf16[3,512,256]{2,1,0:T(8,128)(2,1)S(1)}, u32[]{:S(2)}, u32[]{:S(2)}) collective-permute-start(bf16[3,512,256]{2,1,0:T(8,128)(2,1)} %collective-permute-done.1.refs_0_.refs_8_), channel_id=1, source_target_pairs={{0,4},{4,0},{8,12},{12,8},{16,20},{20,16},{24,28},{28,24},{1,5},{5... | collective-permute-start | bytes 2359304 | tf_op jit(solution)/shard_map/ppermute | solution.py:336
  68.1 13.0 %collective-permute-start.5 = (bf16[3,512,256]{2,1,0:T(8,128)(2,1)}, bf16[3,512,256]{2,1,0:T(8,128)(2,1)S(1)}, u32[]{:S(2)}, u32[]{:S(2)}) collective-permute-start(bf16[3,512,256]{2,1,0:T(8,128)(2,1)} %collective-permute-done.3.refs_1_.refs_9_), channel_id=1, source_target_pairs={{0,4},{4,0},{8,12},{12,8},{16,20},{20,16},{24,28},{28,24},{1,5},{5... | collective-permute-start | bytes 2359304 | tf_op jit(solution)/shard_map/ppermute | solution.py:336
  69.2 42.1 %collective-permute-start.13 = (bf16[3,1024,256]{2,1,0:T(8,128)(2,1)S(1)}, bf16[3,1024,256]{2,1,0:T(8,128)(2,1)S(1)}, u32[]{:S(2)}, u32[]{:S(2)}) collective-permute-start(bf16[3,1024,256]{2,1,0:T(8,128)(2,1)S(1)} %get-tuple-element.27.refs_0_.refs_12_), channel_id=1, source_target_pairs={{0,4},{4,0},{8,12},{12,8},{16,20},{20,16},{24,28},{28,24},{1,5},{5... | collective-permute-start | bytes 4718600 | tf_op jit(solution)/shard_map/ppermute | solution.py:336
  81.1 6.5 %copy-start.6 = (bf16[3,512,256]{2,1,0:T(8,128)(2,1)}, bf16[3,512,256]{2,1,0:T(8,128)(2,1)S(1)}, u32[]{:S(2)}) copy-start(bf16[3,512,256]{2,1,0:T(8,128)(2,1)S(1)} %collective-permute-done.4.refs_2_.refs_10_) | copy-start | bytes 2359300
  81.1 6.5 %copy-start.8 = (bf16[3,512,256]{2,1,0:T(8,128)(2,1)}, bf16[3,512,256]{2,1,0:T(8,128)(2,1)S(1)}, u32[]{:S(2)}) copy-start(bf16[3,512,256]{2,1,0:T(8,128)(2,1)S(1)} %collective-permute-done.5.refs_3_.refs_11_) | copy-start | bytes 2359300
  87.6 19.7 %copy-start.29 = (f32[512]{0:T(512)S(1)}, f32[512]{0:T(512)}, u32[]{:S(2)}) copy-start(f32[512]{0:T(512)} %param.11) | copy-start | bytes 6148
  104.6 6.7 %copy-start.2 = (bf16[3,1024,256]{2,1,0:T(8,128)(2,1)}, bf16[3,1024,256]{2,1,0:T(8,128)(2,1)S(1)}, u32[]{:S(2)}) copy-start(bf16[3,1024,256]{2,1,0:T(8,128)(2,1)S(1)} %collective-permute-done.9.refs_2_.refs_14_) | copy-start | bytes 4718596
  104.6 6.8 %collective-permute-start.14 = (bf16[3,1024,256]{2,1,0:T(8,128)(2,1)S(1)}, bf16[3,1024,256]{2,1,0:T(8,128)(2,1)S(1)}, u32[]{:S(2)}, u32[]{:S(2)}) collective-permute-start(bf16[3,1024,256]{2,1,0:T(8,128)(2,1)S(1)} %collective-permute-done.9.refs_2_.refs_14_), channel_id=1, source_target_pairs={{0,4},{4,0},{8,12},{12,8},{16,20},{20,16},{24,28},{28,24},{1,5},{5... | collective-permute-start | bytes 4718600 | tf_op jit(solution)/shard_map/ppermute | solution.py:336
  105.0 6.3 %copy-start.19 = (bf16[3,1024,256]{2,1,0:T(8,128)(2,1)}, bf16[3,1024,256]{2,1,0:T(8,128)(2,1)S(1)}, u32[]{:S(2)}) copy-start(bf16[3,1024,256]{2,1,0:T(8,128)(2,1)S(1)} %collective-permute-done.10.refs_4_.refs_16_) | copy-start | bytes 4718596
  105.0 6.4 %collective-permute-start.15 = (bf16[3,1024,256]{2,1,0:T(8,128)(2,1)S(1)}, bf16[3,1024,256]{2,1,0:T(8,128)(2,1)}, u32[]{:S(2)}, u32[]{:S(2)}) collective-permute-start(bf16[3,1024,256]{2,1,0:T(8,128)(2,1)S(1)} %collective-permute-done.10.refs_4_.refs_16_), channel_id=1, source_target_pairs={{0,4},{4,0},{8,12},{12,8},{16,20},{20,16},{24,28},{28,24},{1,5},{5... | collective-permute-start | bytes 4718600 | tf_op jit(solution)/shard_map/ppermute | solution.py:336
  105.2 20.0 %collective-permute-start.11 = (bf16[3,512,256]{2,1,0:T(8,128)(2,1)S(1)}, bf16[3,512,256]{2,1,0:T(8,128)(2,1)}, u32[]{:S(2)}, u32[]{:S(2)}) collective-permute-start(bf16[3,512,256]{2,1,0:T(8,128)(2,1)S(1)} %slice.125), channel_id=1, source_target_pairs={{0,16},{4,20},{8,24},{12,28},{16,0},{20,4},{24,8},{28,12},{1,17},{... | collective-permute-start | bytes 2359304 | tf_op jit(solution)/shard_map/ppermute | solution.py:336
  106.8 19.7 %collective-permute-start.12 = (bf16[3,512,256]{2,1,0:T(8,128)(2,1)S(1)}, bf16[3,512,256]{2,1,0:T(8,128)(2,1)}, u32[]{:S(2)}, u32[]{:S(2)}) collective-permute-start(bf16[3,512,256]{2,1,0:T(8,128)(2,1)S(1)} %slice.126), channel_id=1, source_target_pairs={{0,8},{4,12},{8,0},{12,4},{16,24},{20,28},{24,16},{28,20},{1,9},{5... | collective-permute-start | bytes 2359304 | tf_op jit(solution)/shard_map/ppermute | solution.py:336
  111.3 10.9 %copy-start.10 = (bf16[512,768]{1,0:T(8,128)(2,1)}, bf16[512,768]{1,0:T(8,128)(2,1)S(1)}, u32[]{:S(2)}) copy-start(bf16[512,768]{1,0:T(8,128)(2,1)S(1)} %get-tuple-element.32.refs_0_) | copy-start | bytes 2359300
  111.3 10.9 %copy-start.15 = (bf16[512,256]{1,0:T(8,128)(2,1)}, bf16[512,256]{1,0:T(8,128)(2,1)S(1)}, u32[]{:S(2)}) copy-start(bf16[512,256]{1,0:T(8,128)(2,1)S(1)} %get-tuple-element.26) | copy-start | bytes 786436
  111.4 10.9 %copy-start.4 = (bf16[3,1024,256]{2,1,0:T(8,128)(2,1)}, bf16[3,1024,256]{2,1,0:T(8,128)(2,1)S(1)}, u32[]{:S(2)}) copy-start(bf16[3,1024,256]{2,1,0:T(8,128)(2,1)S(1)} %collective-permute-done.13.refs_1_.refs_13_) | copy-start | bytes 4718596
  111.4 1.2 copy-start.20
  122.3 1.1 copy-start.13
  126.5 2.6 collective-permute-start.16
  126.5 3.7 %collective-permute-start.17 = (bf16[3,512,256]{2,1,0:T(8,128)(2,1)}, bf16[3,512,256]{2,1,0:T(8,128)(2,1)}, u32[]{:S(2)}, u32[]{:S(2)}) collective-permute-start(bf16[3,512,256]{2,1,0:T(8,128)(2,1)} %collective-permute-done.12.refs_1_.refs_19_), channel_id=1, source_target_pairs={{0,4},{4,0},{8,12},{12,8},{16,20},{20,16},{24,28},{28,24},{1,5},{5... | collective-permute-start | bytes 2359304 | tf_op jit(solution)/shard_map/ppermute | solution.py:336
  130.2 1.4 copy-start.14
  131.7 19.6 %copy-start.5 = (bf16[3,1024,256]{2,1,0:T(8,128)(2,1)S(1)}, bf16[3,1024,256]{2,1,0:T(8,128)(2,1)}, u32[]{:S(2)}) copy-start(bf16[3,1024,256]{2,1,0:T(8,128)(2,1)} %copy-done.4) | copy-start | bytes 4718596
  131.7 19.6 %copy-start.7 = (bf16[3,512,256]{2,1,0:T(8,128)(2,1)S(1)}, bf16[3,512,256]{2,1,0:T(8,128)(2,1)}, u32[]{:S(2)}) copy-start(bf16[3,512,256]{2,1,0:T(8,128)(2,1)} %copy-done.6) | copy-start | bytes 2359300
  131.7 19.6 %copy-start.9 = (bf16[3,512,256]{2,1,0:T(8,128)(2,1)S(1)}, bf16[3,512,256]{2,1,0:T(8,128)(2,1)}, u32[]{:S(2)}) copy-start(bf16[3,512,256]{2,1,0:T(8,128)(2,1)} %copy-done.8) | copy-start | bytes 2359300
  131.7 19.6 %copy-start.11 = (bf16[512,768]{1,0:T(8,128)(2,1)S(1)}, bf16[512,768]{1,0:T(8,128)(2,1)}, u32[]{:S(2)}) copy-start(bf16[512,768]{1,0:T(8,128)(2,1)} %copy-done.10) | copy-start | bytes 2359300
  138.8 12.5 %copy-start.3 = (bf16[3,1024,256]{2,1,0:T(8,128)(2,1)S(1)}, bf16[3,1024,256]{2,1,0:T(8,128)(2,1)}, u32[]{:S(2)}) copy-start(bf16[3,1024,256]{2,1,0:T(8,128)(2,1)} %copy-done.2) | copy-start | bytes 4718596
  151.3 3.8 %copy-start.17 = (bf16[512,256]{1,0:T(8,128)(2,1)}, bf16[512,256]{1,0:T(8,128)(2,1)S(1)}, u32[]{:S(2)}) copy-start(bf16[512,256]{1,0:T(8,128)(2,1)S(1)} %get-tuple-element.38) | copy-start | bytes 786436
  151.3 8.1 %copy-start.12 = (bf16[512,768]{1,0:T(8,128)(2,1)}, bf16[512,768]{1,0:T(8,128)(2,1)S(1)}, u32[]{:S(2)}) copy-start(bf16[512,768]{1,0:T(8,128)(2,1)S(1)} %get-tuple-element.39.refs_1_) | copy-start | bytes 2359300
  155.1 16.8 %collective-permute-start.18 = (bf16[512,512]{1,0:T(8,128)(2,1)}, bf16[512,512]{1,0:T(8,128)(2,1)}, u32[]{:S(2)}, u32[]{:S(2)}) collective-permute-start(bf16[512,512]{1,0:T(8,128)(2,1)} %input_grad.12), channel_id=1, source_target_pairs={{0,1},{3,2},{4,5},{7,6},{8,9},{11,10},{12,13},{15,14},{16,17},{19,... | collective-permute-start | bytes 1572872 | tf_op jit(solution)/shard_map/ppermute | solution.py:474
  162.8 19.6 %collective-permute-start.19 = (bf16[512,512]{1,0:T(8,128)(2,1)}, bf16[512,512]{1,0:T(8,128)(2,1)S(1)}, u32[]{:S(2)}, u32[]{:S(2)}) collective-permute-start(bf16[512,512]{1,0:T(8,128)(2,1)} %input_grad.13), channel_id=1, source_target_pairs={{0,1},{3,2},{4,5},{7,6},{8,9},{11,10},{12,13},{15,14},{16,17},{19,... | collective-permute-start | bytes 1572872 | tf_op jit(solution)/shard_map/ppermute | solution.py:474
  170.5 34.4 %collective-permute-start.25 = (bf16[512,1024]{1,0:T(8,128)(2,1)}, bf16[512,1024]{1,0:T(8,128)(2,1)S(1)}, u32[]{:S(2)}, u32[]{:S(2)}) collective-permute-start(bf16[512,1024]{1,0:T(8,128)(2,1)} %input_grad.16), channel_id=1, source_target_pairs={{0,1},{3,2},{4,5},{7,6},{8,9},{11,10},{12,13},{15,14},{16,17},{19,... | collective-permute-start | bytes 3145736 | tf_op jit(solution)/shard_map/ppermute | solution.py:474
  184.0 42.4 %collective-permute-start.23 = (bf16[512,1024]{1,0:T(8,128)(2,1)S(1)}, bf16[512,1024]{1,0:T(8,128)(2,1)}, u32[]{:S(2)}, u32[]{:S(2)}) collective-permute-start(bf16[512,1024]{1,0:T(8,128)(2,1)S(1)} %add_convert_fusion.5), channel_id=1, source_target_pairs={{1,2},{2,1},{5,6},{6,5},{9,10},{10,9},{13,14},{14,13},{17,18},{18,... | collective-permute-start | bytes 3145736 | tf_op jit(solution)/shard_map/ppermute | solution.py:474
  186.2 18.6 %copy-start.24 = (bf16[512,1024]{1,0:T(8,128)(2,1)S(1)}, bf16[512,1024]{1,0:T(8,128)(2,1)}, u32[]{:S(2)}) copy-start(bf16[512,1024]{1,0:T(8,128)(2,1)} %input_grad.16) | copy-start | bytes 3145732
  192.7 38.0 %collective-permute-start.20 = (bf16[512,1024]{1,0:T(8,128)(2,1)}, bf16[512,1024]{1,0:T(8,128)(2,1)}, u32[]{:S(2)}, u32[]{:S(2)}) collective-permute-start(bf16[512,1024]{1,0:T(8,128)(2,1)} %input_grad.11), channel_id=1, source_target_pairs={{0,1},{3,2},{4,5},{7,6},{8,9},{11,10},{12,13},{15,14},{16,17},{19,... | collective-permute-start | bytes 3145736 | tf_op jit(solution)/shard_map/ppermute | solution.py:474
  206.3 43.8 %collective-permute-start.28 = (bf16[512,1024]{1,0:T(8,128)(2,1)}, bf16[512,1024]{1,0:T(8,128)(2,1)}, u32[]{:S(2)}, u32[]{:S(2)}) collective-permute-start(bf16[512,1024]{1,0:T(8,128)(2,1)} %add_convert_fusion.1), channel_id=1, source_target_pairs={{1,2},{2,1},{5,6},{6,5},{9,10},{10,9},{13,14},{14,13},{17,18},{18,... | collective-permute-start | bytes 3145736 | tf_op jit(solution)/shard_map/ppermute | solution.py:474
  214.3 6.4 %copy-start.26 = (bf16[512,1024]{1,0:T(8,128)(2,1)S(1)}, bf16[512,1024]{1,0:T(8,128)(2,1)}, u32[]{:S(2)}) copy-start(bf16[512,1024]{1,0:T(8,128)(2,1)} %input_grad.15) | copy-start | bytes 3145732
  220.8 9.9 %copy-start.25 = (bf16[512,1024]{1,0:T(8,128)(2,1)S(1)}, bf16[512,1024]{1,0:T(8,128)(2,1)}, u32[]{:S(2)}) copy-start(bf16[512,1024]{1,0:T(8,128)(2,1)} %input_grad.11) | copy-start | bytes 3145732
  220.8 33.6 %collective-permute-start.26 = (bf16[512,1024]{1,0:T(8,128)(2,1)S(1)}, bf16[512,1024]{1,0:T(8,128)(2,1)}, u32[]{:S(2)}, u32[]{:S(2)}) collective-permute-start(bf16[512,1024]{1,0:T(8,128)(2,1)S(1)} %copy-done.26), channel_id=1, source_target_pairs={{0,1},{3,2},{4,5},{7,6},{8,9},{11,10},{12,13},{15,14},{16,17},{19,... | collective-permute-start | bytes 3145736 | tf_op jit(solution)/shard_map/ppermute | solution.py:474
  229.4 36.7 %collective-permute-start.24 = (bf16[512,1024]{1,0:T(8,128)(2,1)}, bf16[512,1024]{1,0:T(8,128)(2,1)}, u32[]{:S(2)}, u32[]{:S(2)}) collective-permute-start(bf16[512,1024]{1,0:T(8,128)(2,1)} %add_convert_fusion.4), channel_id=1, source_target_pairs={{1,0},{2,3},{5,4},{6,7},{9,8},{10,11},{13,12},{14,15},{17,16},{18,... | collective-permute-start | bytes 3145736 | tf_op jit(solution)/shard_map/ppermute | solution.py:474
  233.3 38.6 %collective-permute-start.22 = (bf16[512,1024]{1,0:T(8,128)(2,1)}, bf16[512,1024]{1,0:T(8,128)(2,1)}, u32[]{:S(2)}, u32[]{:S(2)}) collective-permute-start(bf16[512,1024]{1,0:T(8,128)(2,1)} %add_convert_fusion.6), channel_id=1, source_target_pairs={{1,2},{2,1},{5,6},{6,5},{9,10},{10,9},{13,14},{14,13},{17,18},{18,... | collective-permute-start | bytes 3145736 | tf_op jit(solution)/shard_map/ppermute | solution.py:474
  234.9 6.4 %copy-start.22 = (bf16[512,1024]{1,0:T(8,128)(2,1)S(1)}, bf16[512,1024]{1,0:T(8,128)(2,1)}, u32[]{:S(2)}) copy-start(bf16[512,1024]{1,0:T(8,128)(2,1)} %input_grad.10) | copy-start | bytes 3145732
  241.4 39.1 %collective-permute-start.21 = (bf16[512,1024]{1,0:T(8,128)(2,1)S(1)}, bf16[512,1024]{1,0:T(8,128)(2,1)}, u32[]{:S(2)}, u32[]{:S(2)}) collective-permute-start(bf16[512,1024]{1,0:T(8,128)(2,1)S(1)} %copy-done.22), channel_id=1, source_target_pairs={{0,1},{3,2},{4,5},{7,6},{8,9},{11,10},{12,13},{15,14},{16,17},{19,... | collective-permute-start | bytes 3145736 | tf_op jit(solution)/shard_map/ppermute | solution.py:474
  253.1 40.7 %collective-permute-start.29 = (bf16[512,1024]{1,0:T(8,128)(2,1)}, bf16[512,1024]{1,0:T(8,128)(2,1)}, u32[]{:S(2)}, u32[]{:S(2)}) collective-permute-start(bf16[512,1024]{1,0:T(8,128)(2,1)} %add_convert_fusion), channel_id=1, source_target_pairs={{1,0},{2,3},{5,4},{6,7},{9,8},{10,11},{13,12},{14,15},{17,16},{18,... | collective-permute-start | bytes 3145736 | tf_op jit(solution)/shard_map/ppermute | solution.py:474
  257.1 36.7 %collective-permute-start.27 = (bf16[512,1024]{1,0:T(8,128)(2,1)}, bf16[512,1024]{1,0:T(8,128)(2,1)}, u32[]{:S(2)}, u32[]{:S(2)}) collective-permute-start(bf16[512,1024]{1,0:T(8,128)(2,1)} %add_convert_fusion.2), channel_id=1, source_target_pairs={{1,2},{2,1},{5,6},{6,5},{9,10},{10,9},{13,14},{14,13},{17,18},{18,... | collective-permute-start | bytes 3145736 | tf_op jit(solution)/shard_map/ppermute | solution.py:474
  258.8 6.4 %copy-start.21 = (bf16[512,1024]{1,0:T(8,128)(2,1)S(1)}, bf16[512,1024]{1,0:T(8,128)(2,1)}, u32[]{:S(2)}) copy-start(bf16[512,1024]{1,0:T(8,128)(2,1)} %input_grad.17) | copy-start | bytes 3145732
  265.2 8.1 %copy-start.16 = (bf16[512,256]{1,0:T(8,128)(2,1)S(1)}, bf16[512,256]{1,0:T(8,128)(2,1)}, u32[]{:S(2)}) copy-start(bf16[512,256]{1,0:T(8,128)(2,1)} %copy-done.15) | copy-start | bytes 786436
  265.2 8.1 %copy-start.18 = (bf16[512,256]{1,0:T(8,128)(2,1)S(1)}, bf16[512,256]{1,0:T(8,128)(2,1)}, u32[]{:S(2)}) copy-start(bf16[512,256]{1,0:T(8,128)(2,1)} %copy-done.17) | copy-start | bytes 786436
  266.1 18.5 %collective-permute-start.30 = (bf16[512,512]{1,0:T(8,128)(2,1)}, bf16[512,512]{1,0:T(8,128)(2,1)S(1)}, u32[]{:S(2)}, u32[]{:S(2)}) collective-permute-start(bf16[512,512]{1,0:T(8,128)(2,1)} %get-tuple-element.48), channel_id=1, source_target_pairs={{0,1},{3,2},{4,5},{7,6},{8,9},{11,10},{12,13},{15,14},{16,17},{19,... | collective-permute-start | bytes 1572872 | tf_op jit(solution)/shard_map/ppermute | solution.py:474
  271.9 21.9 %collective-permute-start.31 = (bf16[512,512]{1,0:T(8,128)(2,1)S(1)}, bf16[512,512]{1,0:T(8,128)(2,1)S(1)}, u32[]{:S(2)}, u32[]{:S(2)}) collective-permute-start(bf16[512,512]{1,0:T(8,128)(2,1)S(1)} %get-tuple-element.49), channel_id=1, source_target_pairs={{0,1},{3,2},{4,5},{7,6},{8,9},{11,10},{12,13},{15,14},{16,17},{19,... | collective-permute-start | bytes 1572872 | tf_op jit(solution)/shard_map/ppermute | solution.py:474
  280.4 13.4 %copy-start.23 = (bf16[512,1024]{1,0:T(8,128)(2,1)S(1)}, bf16[512,1024]{1,0:T(8,128)(2,1)}, u32[]{:S(2)}) copy-start(bf16[512,1024]{1,0:T(8,128)(2,1)} %input_grad.14) | copy-start | bytes 3145732

commit v2 on v1

--- a/solution.py
+++ b/solution.py
@@ -504,12 +504,16 @@
         last = part(3, core)
         back = send(add(parts[2][core], swapped[1][core]), outwards)
         if core:
-            rest = [last, swapped[2][core], back]
+            rest = add(last, swapped[2][core], back)
             half = last.shape[1] // 2
-            out += [add(*[a[:, i * half : (i + 1) * half] for a in rest], got[2][core][i]) for i in range(2)]
+            out.append(add(rest[:, :half], got[2][core][0]))
+            rest = rest[:, half:]
         else:
             out.append(add(last, got[2][core], swapped[2][core], back))
-    return (jnp.concatenate(gated, axis=1), jnp.concatenate(out, axis=1))
+    base = jnp.pad(jnp.concatenate(out, axis=1), ((0, 0), (0, half)))
+    base, rest = lax.optimization_barrier((base, rest))
+    end = add(rest, got[2][1][1])
+    return (jnp.concatenate(gated, axis=1), lax.dynamic_update_slice(base, end, (0, 3 * half)))
 
 
 def solution(mesh):

time: 299 us -> 302 us (1.010)
  waiting for transfers between devices: 81.7 us -> 86 us
    ppermute x14, waiting for transfers between devices: 25 us -> 29.3 us  [send(): return lax.ppermute(block, 'chan', pairs)]
    unnamed x61 -> x65, local copies, waits for them, and re-layouts: 4.95 us -> 6.27 us
    convert_element_type x8 -> x9, other arithmetic: 19.4 us -> 19.2 us  [add(): return sum((t.astype(jnp.float32) for t in terms)).astype(jnp.bfloat16)]
  transfers between devices with their start and end apart: 32 -> 32, of which waited for: 12 -> 13; matrix products, arithmetic and copies ran while one was open for 9% -> 9% of each run, Pallas kernels for 27% -> 26%
where the time goes in v2:
time: 302 us; the launch traced here: 301 us
  Pallas kernels  93.9 us (31%)
  waiting for transfers between devices  86 us (28%)
  starting transfers between devices  56.2 us (19%)
  blocking collectives  25.4 us (8%)
  other arithmetic  20.4 us (7%)
  local copies, waits for them, and re-layouts  15.3 us (5%)
  between operations  3.88 us (1%)
    ppermute x18, waiting for transfers between devices, exchange(): return lax.ppermute(array, axis, [(i, i ^ bit) for i in range(count)])  56.7 us
    pallas_call x9, Pallas kernels, input_grad(): pl.pallas_call(functools.partial(input_grad_kernel, halves, half), grid_s...  51.4 us
    ppermute x14, starting transfers between devices, send(): return lax.ppermute(block, 'chan', pairs)  43.8 us
    ppermute x14, waiting for transfers between devices, send(): return lax.ppermute(block, 'chan', pairs)  29.3 us
    all_gather x2, blocking collectives, meet(): return lax.all_gather(jnp.concatenate([m[2] for m in made], axis=2), 'seq')  25.4 us
    pallas_call x2, Pallas kernels, project_part(): pl.pallas_call(functools.partial(project_part_kernel, halves), grid_spec=...  20.9 us
    convert_element_type x9, other arithmetic, add(): return sum((t.astype(jnp.float32) for t in terms)).astype(jnp.bfloat16)  19.2 us
    pallas_call x2, Pallas kernels, project(): pl.pallas_call(functools.partial(project_kernel, rows // SUBS, halves), g...  13.6 us
  transfers between devices with their start and end apart: 32, of which 13 were waited for; matrix products, arithmetic and copies ran while one was open for 9% of the time, Pallas kernels for 26%

profile of v2, /device:TPU:0, one launch (start us, length us, event | category | flops | bytes accessed | tf_op | source)
XLA Modules:
  0.0 301.1 jit_solution(18077969440329953438)
XLA Ops:
  0.6 2.1 fusion.4
  2.8 3.0 collective-permute-start
  5.8 1.5 collective-permute-start.2
  7.3 33.0 %collective-permute-done.refs_2_.refs_4_ = bf16[3,1024,256]{2,1,0:T(8,128)(2,1)} collective-permute-done((bf16[3,1024,256]{2,1,0:T(8,128)(2,1)S(1)}, bf16[3,1024,256]{2,1,0:T(8,128)(2,1)}, u32[]{:S(2)}, u32[]{:S(2)}) %collective-permute-start) | collective-permute-done | bytes 1572896 | tf_op jit(solution)/shard_map/ppermute | solution.py:336
  40.3 1.5 collective-permute-done.2.refs_4_.refs_6_
  41.7 2.1 slice.104
  43.8 1.5 collective-permute-start.1
  45.3 2.1 slice.105
  48.2 1.3 collective-permute-start.9
  50.1 14.3 %collective-permute-done.1.refs_0_.refs_8_ = bf16[3,512,256]{2,1,0:T(8,128)(2,1)} collective-permute-done((bf16[3,512,256]{2,1,0:T(8,128)(2,1)}, bf16[3,512,256]{2,1,0:T(8,128)(2,1)}, u32[]{:S(2)}, u32[]{:S(2)}) %collective-permute-start.1) | collective-permute-done | bytes 786464 | tf_op jit(solution)/shard_map/ppermute | solution.py:336
  64.5 3.6 %collective-permute-done.3.refs_1_.refs_9_ = bf16[3,512,256]{2,1,0:T(8,128)(2,1)} collective-permute-done((bf16[3,512,256]{2,1,0:T(8,128)(2,1)}, bf16[3,512,256]{2,1,0:T(8,128)(2,1)}, u32[]{:S(2)}, u32[]{:S(2)}) %collective-permute-start.3) | collective-permute-done | bytes 786464 | tf_op jit(solution)/shard_map/ppermute | solution.py:336
  69.8 11.2 %project_part.2.refs_4_ = f32[512,768]{1,0:T(8,128)S(1)} custom-call(s32[6]{0:T(128)S(1)} %bitcast.28, bf16[512,8192]{1,0:T(8,128)(2,1)} %x_ref.7, bf16[3,1024,256]{2,1,0:T(8,128)(2,1)S(1)} %get-tuple-element.48.refs_0_.refs_2_, bf16[3,1024,256]{2,1,0:T(8,128)(2,1)} %collective-permute-done.6.refs_1_.refs_3_, ...), custom_call_target="tpu_custom_call" | custom-call | flops 4831838208 | bytes 15728640 | tf_op jit(solution)/shard_map/project_part/pallas_call | solution.py:186
  81.1 6.5 %project.2 = (bf16[3,512,256]{2,1,0:T(8,128)(2,1)S(1)}, f32[2,2,128,128]{3,2,1,0:T(8,128)S(1)}, f32[2,16,256]{2,1,0:T(8,128)S(1)}) custom-call(s32[2]{0:T(128)S(1)} %slice.81.order_ref, bf16[512,8192]{1,0:T(8,128)(2,1)} %x_ref.7, bf16[3,512,256]{2,1,0:T(8,128)(2,1)} %collective-permute-done.1.refs_0_.refs_8_, ...), custom_call_target="tpu_custom_call" | custom-call | flops 1610612736 | bytes 5242880 | tf_op jit(solution)/shard_map/project/pallas_call | solution.py:208
  87.6 17.0 %all-gather = f32[16,16,256]{2,1,0:T(8,128)S(1)} all-gather(f32[2,16,256]{2,1,0:T(8,128)S(1)} %get-tuple-element.27), channel_id=2, replica_groups=mesh['seq'=8,'chan'=4] {'seq'}, dimensions={0}, use_global_device_ids=true | all-gather | bytes 294912 | tf_op jit(solution)/shard_map/all_gather | solution.py:414
  105.2 1.6 collective-permute-start.11
  107.3 4.0 %scan.2 = (bf16[512,256]{1,0:T(8,128)(2,1)S(1)}, bf16[512,768]{1,0:T(8,128)(2,1)S(1)}) custom-call(s32[1]{0:T(128)} %bitcast.place_ref, bf16[3,512,256]{2,1,0:T(8,128)(2,1)S(1)} %get-tuple-element.25.proj_ref, bf16[512,256]{1,0:T(8,128)(2,1)S(1)} %get-tuple-element.53.refs_5_.g_ref, f32[4,16,256]{2,1,0:T(8,128)S(1)} %get-tuple-element.55.refs_6_.coef_ref, ...), custom_call_target="tpu_custom_call" | custom-call | flops 33554432 | bytes 1572864 | tf_op jit(solution)/shard_map/scan/pallas_call | solution.py:239
  111.4 1.2 copy-done.20
  112.6 9.7 %project_part.3.refs_4_ = f32[512,768]{1,0:T(8,128)S(1)} custom-call(s32[6]{0:T(128)S(1)} %bitcast.29, bf16[512,8192]{1,0:T(8,128)(2,1)} %x_ref.7, bf16[3,1024,256]{2,1,0:T(8,128)(2,1)S(1)} %get-tuple-element.29.refs_0_.refs_12_, bf16[3,1024,256]{2,1,0:T(8,128)(2,1)S(1)} %collective-permute-done.13.refs_1_.refs_13_, bf16[3,1024,256]{2,1,0:T(8,128)(2,1)} %copy-done.2, ...), custom_call_target="tpu_custom_call" | custom-call | flops 4831838208 | bytes 15728640 | tf_op jit(solution)/shard_map/project_part/pallas_call | solution.py:186
  122.3 1.1 copy-done.13
  123.4 1.8 collective-permute-done.11.refs_0_.refs_18_
  125.3 1.2 collective-permute-done.12.refs_1_.refs_19_
  129.1 1.1 collective-permute-done.17.refs_3_.refs_21_
  130.2 1.4 copy-done.14
  131.7 7.1 %project.3 = (bf16[3,512,256]{2,1,0:T(8,128)(2,1)S(1)}, f32[2,2,128,128]{3,2,1,0:T(8,128)S(1)}, f32[2,16,256]{2,1,0:T(8,128)S(1)}) custom-call(s32[2]{0:T(128)S(1)} %slice.81.order_ref, bf16[512,8192]{1,0:T(8,128)(2,1)} %x_ref.7, bf16[3,512,256]{2,1,0:T(8,128)(2,1)} %collective-permute-done.11.refs_0_.refs_18_, ...), custom_call_target="tpu_custom_call" | custom-call | flops 1610612736 | bytes 5242880 | tf_op jit(solution)/shard_map/project/pallas_call | solution.py:208
  138.8 8.5 %all-gather.1 = f32[16,16,256]{2,1,0:T(8,128)S(1)} all-gather(f32[2,16,256]{2,1,0:T(8,128)S(1)} %get-tuple-element.39), channel_id=3, replica_groups=mesh['seq'=8,'chan'=4] {'seq'}, dimensions={0}, use_global_device_ids=true | all-gather | bytes 294912 | tf_op jit(solution)/shard_map/all_gather | solution.py:414
  147.3 4.0 %scan.3 = (bf16[512,256]{1,0:T(8,128)(2,1)S(1)}, bf16[512,768]{1,0:T(8,128)(2,1)S(1)}) custom-call(s32[1]{0:T(128)} %bitcast.place_ref, bf16[3,512,256]{2,1,0:T(8,128)(2,1)S(1)} %get-tuple-element.37.proj_ref, bf16[512,256]{1,0:T(8,128)(2,1)S(1)} %get-tuple-element.52.refs_5_.g_ref, f32[4,16,256]{2,1,0:T(8,128)S(1)} %get-tuple-element.54.refs_6_.coef_ref, ...), custom_call_target="tpu_custom_call" | custom-call | flops 33554432 | bytes 1572864 | tf_op jit(solution)/shard_map/scan/pallas_call | solution.py:239
  151.3 3.7 %input_grad.12 = bf16[512,512]{1,0:T(8,128)(2,1)} custom-call(s32[1]{0:T(128)} %bitcast.16.pick_ref, bf16[512,768]{1,0:T(8,128)(2,1)S(1)} %copy-done.11, bf16[512,768]{1,0:T(8,128)(2,1)S(1)} %get-tuple-element.41.refs_1_, bf16[3,1024,256]{2,1,0:T(8,128)(2,1)S(1)} %get-tuple-element.48.refs_0_.refs_2_, ...), custom_call_target="tpu_custom_call" | custom-call | flops 805306368 | bytes 3670016 | tf_op jit(solution)/shard_map/input_grad/pallas_call | solution.py:313
  155.1 4.3 %collective-permute-start.18 = (bf16[512,512]{1,0:T(8,128)(2,1)}, bf16[512,512]{1,0:T(8,128)(2,1)}, u32[]{:S(2)}, u32[]{:S(2)}) collective-permute-start(bf16[512,512]{1,0:T(8,128)(2,1)} %input_grad.12), channel_id=1, source_target_pairs={{0,1},{3,2},{4,5},{7,6},{8,9},{11,10},{12,13},{15,14},{16,17},{19,... | collective-permute-start | bytes 1572872 | tf_op jit(solution)/shard_map/ppermute | solution.py:474
  159.4 3.4 %input_grad.13 = bf16[512,512]{1,0:T(8,128)(2,1)} custom-call(s32[1]{0:T(128)} %bitcast.16.pick_ref, bf16[512,768]{1,0:T(8,128)(2,1)S(1)} %copy-done.11, bf16[512,768]{1,0:T(8,128)(2,1)S(1)} %get-tuple-element.41.refs_1_, bf16[3,1024,256]{2,1,0:T(8,128)(2,1)S(1)} %get-tuple-element.48.refs_0_.refs_2_, ...), custom_call_target="tpu_custom_call" | custom-call | flops 805306368 | bytes 3670016 | tf_op jit(solution)/shard_map/input_grad/pallas_call | solution.py:313
  162.8 1.3 collective-permute-start.19
  164.2 6.3 %input_grad.16 = bf16[512,1024]{1,0:T(8,128)(2,1)} custom-call(s32[1]{0:T(128)} %bitcast.19.pick_ref, bf16[512,768]{1,0:T(8,128)(2,1)} %copy-done.10, bf16[512,768]{1,0:T(8,128)(2,1)} %copy-done.12, bf16[3,1024,256]{2,1,0:T(8,128)(2,1)} %copy-done, bf16[3,1024,256]{2,1,0:T(8,128)(2,1)} %collective-permute-done.6.refs_1_.refs_3_, ...), custom_call_target="tpu_custom_call" | custom-call | flops 1610612736 | bytes 5767168 | tf_op jit(solution)/shard_map/input_grad/pallas_call | solution.py:313
  170.5 1.4 collective-permute-start.25
  171.9 1.1 constant_dynamic-update-slice_fusion.1
  173.0 9.4 %collective-permute-done.19 = bf16[512,512]{1,0:T(8,128)(2,1)S(1)} collective-permute-done((bf16[512,512]{1,0:T(8,128)(2,1)}, bf16[512,512]{1,0:T(8,128)(2,1)S(1)}, u32[]{:S(2)}, u32[]{:S(2)}) %collective-permute-start.19) | collective-permute-done | bytes 524320 | tf_op jit(solution)/shard_map/ppermute | solution.py:474
  182.5 1.6 add_convert_fusion.6
  184.0 1.6 collective-permute-start.23
  187.6 6.4 %input_grad.11 = bf16[512,1024]{1,0:T(8,128)(2,1)} custom-call(s32[1]{0:T(128)} %bitcast.14.pick_ref, bf16[512,768]{1,0:T(8,128)(2,1)} %copy-done.10, bf16[512,768]{1,0:T(8,128)(2,1)} %copy-done.12, bf16[3,1024,256]{2,1,0:T(8,128)(2,1)} %copy-done, bf16[3,1024,256]{2,1,0:T(8,128)(2,1)} %collective-permute-done.6.refs_1_.refs_3_, ...), custom_call_target="tpu_custom_call" | custom-call | flops 1610612736 | bytes 5767168 | tf_op jit(solution)/shard_map/input_grad/pallas_call | solution.py:313
  194.0 5.6 %collective-permute-start.20 = (bf16[512,1024]{1,0:T(8,128)(2,1)}, bf16[512,1024]{1,0:T(8,128)(2,1)}, u32[]{:S(2)}, u32[]{:S(2)}) collective-permute-start(bf16[512,1024]{1,0:T(8,128)(2,1)} %input_grad.11), channel_id=1, source_target_pairs={{0,1},{3,2},{4,5},{7,6},{8,9},{11,10},{12,13},{15,14},{16,17},{19,... | collective-permute-start | bytes 3145736 | tf_op jit(solution)/shard_map/ppermute | solution.py:474
  199.6 5.3 %collective-permute-done.25 = bf16[512,1024]{1,0:T(8,128)(2,1)S(1)} collective-permute-done((bf16[512,1024]{1,0:T(8,128)(2,1)}, bf16[512,1024]{1,0:T(8,128)(2,1)S(1)}, u32[]{:S(2)}, u32[]{:S(2)}) %collective-permute-start.25) | collective-permute-done | bytes 1048608 | tf_op jit(solution)/shard_map/ppermute | solution.py:474
  204.9 1.5 add_convert_fusion.2
  206.4 1.6 collective-permute-start.28
  208.0 6.3 %input_grad.17 = bf16[512,1024]{1,0:T(8,128)(2,1)} custom-call(s32[1]{0:T(128)} %bitcast.20.pick_ref, bf16[512,768]{1,0:T(8,128)(2,1)} %copy-done.10, bf16[512,768]{1,0:T(8,128)(2,1)} %copy-done.12, bf16[3,1024,256]{2,1,0:T(8,128)(2,1)} %copy-done, bf16[3,1024,256]{2,1,0:T(8,128)(2,1)} %collective-permute-done.6.refs_1_.refs_3_, ...), custom_call_target="tpu_custom_call" | custom-call | flops 1610612736 | bytes 5767168 | tf_op jit(solution)/shard_map/input_grad/pallas_call | solution.py:313
  214.3 6.3 %input_grad.15 = bf16[512,1024]{1,0:T(8,128)(2,1)} custom-call(s32[1]{0:T(128)} %bitcast.18.pick_ref, bf16[512,768]{1,0:T(8,128)(2,1)} %copy-done.10, bf16[512,768]{1,0:T(8,128)(2,1)} %copy-done.12, bf16[3,1024,256]{2,1,0:T(8,128)(2,1)} %copy-done, bf16[3,1024,256]{2,1,0:T(8,128)(2,1)} %collective-permute-done.6.refs_1_.refs_3_, ...), custom_call_target="tpu_custom_call" | custom-call | flops 1610612736 | bytes 5767168 | tf_op jit(solution)/shard_map/input_grad/pallas_call | solution.py:313
  220.6 5.5 %collective-permute-start.26 = (bf16[512,1024]{1,0:T(8,128)(2,1)}, bf16[512,1024]{1,0:T(8,128)(2,1)}, u32[]{:S(2)}, u32[]{:S(2)}) collective-permute-start(bf16[512,1024]{1,0:T(8,128)(2,1)} %input_grad.15), channel_id=1, source_target_pairs={{0,1},{3,2},{4,5},{7,6},{8,9},{11,10},{12,13},{15,14},{16,17},{19,... | collective-permute-start | bytes 3145736 | tf_op jit(solution)/shard_map/ppermute | solution.py:474
  226.2 6.3 %input_grad.10 = bf16[512,1024]{1,0:T(8,128)(2,1)} custom-call(s32[1]{0:T(128)} %bitcast.12.pick_ref, bf16[512,768]{1,0:T(8,128)(2,1)} %copy-done.10, bf16[512,768]{1,0:T(8,128)(2,1)} %copy-done.12, bf16[3,1024,256]{2,1,0:T(8,128)(2,1)} %copy-done, bf16[3,1024,256]{2,1,0:T(8,128)(2,1)} %collective-permute-done.6.refs_1_.refs_3_, ...), custom_call_target="tpu_custom_call" | custom-call | flops 1610612736 | bytes 5767168 | tf_op jit(solution)/shard_map/input_grad/pallas_call | solution.py:313
  232.5 3.0 %add_convert_fusion.5 = bf16[512,1024]{1,0:T(8,128)(2,1)} fusion(bf16[512,1024]{1,0:T(8,128)(2,1)} %collective-permute-done.23, bf16[512,1024]{1,0:T(8,128)(2,1)} %input_grad.10), kind=kLoop, calls=%fused_computation.9 | loop fusion | flops 2097152 | bytes 3145728 | tf_op jit(solution)/shard_map/convert_element_type | solution.py:469
  235.6 1.4 collective-permute-start.24
  237.0 2.6 add_convert_fusion.7
  239.6 1.8 collective-permute-start.22
  241.4 8.8 %collective-permute-start.21 = (bf16[512,1024]{1,0:T(8,128)(2,1)S(1)}, bf16[512,1024]{1,0:T(8,128)(2,1)}, u32[]{:S(2)}, u32[]{:S(2)}) collective-permute-start(bf16[512,1024]{1,0:T(8,128)(2,1)S(1)} %copy-done.22), channel_id=1, source_target_pairs={{0,1},{3,2},{4,5},{7,6},{8,9},{11,10},{12,13},{15,14},{16,17},{19,... | collective-permute-start | bytes 3145736 | tf_op jit(solution)/shard_map/ppermute | solution.py:474
  250.2 2.7 add_convert_fusion.1
  252.9 1.4 collective-permute-start.29
  254.4 2.6 add_convert_fusion.3
  257.0 1.6 collective-permute-start.27
  259.5 6.3 %input_grad.14 = bf16[512,1024]{1,0:T(8,128)(2,1)} custom-call(s32[1]{0:T(128)} %bitcast.17.pick_ref, bf16[512,768]{1,0:T(8,128)(2,1)} %copy-done.10, bf16[512,768]{1,0:T(8,128)(2,1)} %copy-done.12, bf16[3,1024,256]{2,1,0:T(8,128)(2,1)} %copy-done, bf16[3,1024,256]{2,1,0:T(8,128)(2,1)} %collective-permute-done.6.refs_1_.refs_3_, ...), custom_call_target="tpu_custom_call" | custom-call | flops 1610612736 | bytes 5767168 | tf_op jit(solution)/shard_map/input_grad/pallas_call | solution.py:313
  265.8 6.3 %input_grad.9 = bf16[512,1024]{1,0:T(8,128)(2,1)} custom-call(s32[1]{0:T(128)} %bitcast.10.pick_ref, bf16[512,768]{1,0:T(8,128)(2,1)} %copy-done.10, bf16[512,768]{1,0:T(8,128)(2,1)} %copy-done.12, bf16[3,1024,256]{2,1,0:T(8,128)(2,1)} %copy-done, bf16[3,1024,256]{2,1,0:T(8,128)(2,1)} %collective-permute-done.6.refs_1_.refs_3_, ...), custom_call_target="tpu_custom_call" | custom-call | flops 1610612736 | bytes 5767168 | tf_op jit(solution)/shard_map/input_grad/pallas_call | solution.py:313
  272.2 6.0 %collective-permute-start.30 = (bf16[512,512]{1,0:T(8,128)(2,1)S(1)}, bf16[512,512]{1,0:T(8,128)(2,1)S(1)}, u32[]{:S(2)}, u32[]{:S(2)}) collective-permute-start(bf16[512,512]{1,0:T(8,128)(2,1)S(1)} %get-tuple-element.51), channel_id=1, source_target_pairs={{0,1},{3,2},{4,5},{7,6},{8,9},{11,10},{12,13},{15,14},{16,17},{19,... | collective-permute-start | bytes 1572872 | tf_op jit(solution)/shard_map/ppermute | solution.py:474
  278.2 1.5 collective-permute-start.31
  279.7 2.8 add_convert_fusion.4
  282.5 3.3 %collective-permute-done.29 = bf16[512,1024]{1,0:T(8,128)(2,1)} collective-permute-done((bf16[512,1024]{1,0:T(8,128)(2,1)}, bf16[512,1024]{1,0:T(8,128)(2,1)}, u32[]{:S(2)}, u32[]{:S(2)}) %collective-permute-start.29) | collective-permute-done | bytes 1048608 | tf_op jit(solution)/shard_map/ppermute | solution.py:474
  285.7 2.2 add_convert_fusion
  287.9 2.6 collective-permute-done.30
  290.9 8.7 %collective-permute-done.31 = bf16[512,512]{1,0:T(8,128)(2,1)S(1)} collective-permute-done((bf16[512,512]{1,0:T(8,128)(2,1)S(1)}, bf16[512,512]{1,0:T(8,128)(2,1)S(1)}, u32[]{:S(2)}, u32[]{:S(2)}) %collective-permute-start.31) | collective-permute-done | bytes 524320 | tf_op jit(solution)/shard_map/ppermute | solution.py:474
  299.8 1.3 copy-done.28
  (111 shorter events, 7.9 us)
Async XLA Ops:
  2.7 156.6 %copy-start = (bf16[3,1024,256]{2,1,0:T(8,128)(2,1)}, bf16[3,1024,256]{2,1,0:T(8,128)(2,1)S(1)}, u32[]{:S(2)}) copy-start(bf16[3,1024,256]{2,1,0:T(8,128)(2,1)S(1)} %get-tuple-element.48.refs_0_.refs_2_) | copy-start | bytes 4718596
  2.7 156.6 %copy-start.1 = (bf16[3,1024,256]{2,1,0:T(8,128)(2,1)}, bf16[3,1024,256]{2,1,0:T(8,128)(2,1)S(1)}, u32[]{:S(2)}) copy-start(bf16[3,1024,256]{2,1,0:T(8,128)(2,1)S(1)} %get-tuple-element.29.refs_0_.refs_12_) | copy-start | bytes 4718596
  2.7 47.3 %copy-start.29 = (f32[16,512]{1,0:T(8,128)S(1)}, f32[16,512]{1,0:T(8,128)}, u32[]{:S(2)}) copy-start(f32[16,512]{1,0:T(8,128)} %param.10) | copy-start | bytes 98308
  2.8 47.3 %copy-start.30 = (f32[16,512]{1,0:T(8,128)S(1)}, f32[16,512]{1,0:T(8,128)}, u32[]{:S(2)}) copy-start(f32[16,512]{1,0:T(8,128)} %param.9) | copy-start | bytes 98308
  2.8 37.5 %collective-permute-start = (bf16[3,1024,256]{2,1,0:T(8,128)(2,1)S(1)}, bf16[3,1024,256]{2,1,0:T(8,128)(2,1)}, u32[]{:S(2)}, u32[]{:S(2)}) collective-permute-start(bf16[3,1024,256]{2,1,0:T(8,128)(2,1)S(1)} %get-tuple-element.48.refs_0_.refs_2_), channel_id=1, source_target_pairs={{0,8},{4,12},{8,0},{12,4},{16,24},{20,28},{24,16},{28,20},{1,9},{5... | collective-permute-start | bytes 4718600 | tf_op jit(solution)/shard_map/ppermute | solution.py:336
  5.8 36.0 %collective-permute-start.2 = (bf16[3,1024,256]{2,1,0:T(8,128)(2,1)S(1)}, bf16[3,1024,256]{2,1,0:T(8,128)(2,1)}, u32[]{:S(2)}, u32[]{:S(2)}) collective-permute-start(bf16[3,1024,256]{2,1,0:T(8,128)(2,1)S(1)} %get-tuple-element.48.refs_0_.refs_2_), channel_id=1, source_target_pairs={{0,16},{4,20},{8,24},{12,28},{16,0},{20,4},{24,8},{28,12},{1,17},{... | collective-permute-start | bytes 4718600 | tf_op jit(solution)/shard_map/ppermute | solution.py:336
  7.3 40.9 %collective-permute-start.6 = (bf16[3,1024,256]{2,1,0:T(8,128)(2,1)S(1)}, bf16[3,1024,256]{2,1,0:T(8,128)(2,1)}, u32[]{:S(2)}, u32[]{:S(2)}) collective-permute-start(bf16[3,1024,256]{2,1,0:T(8,128)(2,1)S(1)} %get-tuple-element.48.refs_0_.refs_2_), channel_id=1, source_target_pairs={{0,4},{4,0},{8,12},{12,8},{16,20},{20,16},{24,28},{28,24},{1,5},{5... | collective-permute-start | bytes 4718600 | tf_op jit(solution)/shard_map/ppermute | solution.py:336
  40.3 7.9 %collective-permute-start.7 = (bf16[3,1024,256]{2,1,0:T(8,128)(2,1)}, bf16[3,1024,256]{2,1,0:T(8,128)(2,1)}, u32[]{:S(2)}, u32[]{:S(2)}) collective-permute-start(bf16[3,1024,256]{2,1,0:T(8,128)(2,1)} %collective-permute-done.refs_2_.refs_4_), channel_id=1, source_target_pairs={{0,4},{4,0},{8,12},{12,8},{16,20},{20,16},{24,28},{28,24},{1,5},{5... | collective-permute-start | bytes 4718600 | tf_op jit(solution)/shard_map/ppermute | solution.py:336
  41.7 6.5 %collective-permute-start.8 = (bf16[3,1024,256]{2,1,0:T(8,128)(2,1)}, bf16[3,1024,256]{2,1,0:T(8,128)(2,1)}, u32[]{:S(2)}, u32[]{:S(2)}) collective-permute-start(bf16[3,1024,256]{2,1,0:T(8,128)(2,1)} %collective-permute-done.2.refs_4_.refs_6_), channel_id=1, source_target_pairs={{0,4},{4,0},{8,12},{12,8},{16,20},{20,16},{24,28},{28,24},{1,5},{5... | collective-permute-start | bytes 4718600 | tf_op jit(solution)/shard_map/ppermute | solution.py:336
  43.8 20.7 %collective-permute-start.1 = (bf16[3,512,256]{2,1,0:T(8,128)(2,1)}, bf16[3,512,256]{2,1,0:T(8,128)(2,1)}, u32[]{:S(2)}, u32[]{:S(2)}) collective-permute-start(bf16[3,512,256]{2,1,0:T(8,128)(2,1)} %slice.104), channel_id=1, source_target_pairs={{0,16},{4,20},{8,24},{12,28},{16,0},{20,4},{24,8},{28,12},{1,17},{... | collective-permute-start | bytes 2359304 | tf_op jit(solution)/shard_map/ppermute | solution.py:336
  47.4 20.7 %collective-permute-start.3 = (bf16[3,512,256]{2,1,0:T(8,128)(2,1)}, bf16[3,512,256]{2,1,0:T(8,128)(2,1)}, u32[]{:S(2)}, u32[]{:S(2)}) collective-permute-start(bf16[3,512,256]{2,1,0:T(8,128)(2,1)} %slice.105), channel_id=1, source_target_pairs={{0,8},{4,12},{8,0},{12,4},{16,24},{20,28},{24,16},{28,20},{1,9},{5... | collective-permute-start | bytes 2359304 | tf_op jit(solution)/shard_map/ppermute | solution.py:336
  48.2 56.4 %collective-permute-start.9 = (bf16[3,1024,256]{2,1,0:T(8,128)(2,1)S(1)}, bf16[3,1024,256]{2,1,0:T(8,128)(2,1)S(1)}, u32[]{:S(2)}, u32[]{:S(2)}) collective-permute-start(bf16[3,1024,256]{2,1,0:T(8,128)(2,1)S(1)} %get-tuple-element.29.refs_0_.refs_12_), channel_id=1, source_target_pairs={{0,8},{4,12},{8,0},{12,4},{16,24},{20,28},{24,16},{28,20},{1,9},{5... | collective-permute-start | bytes 4718600 | tf_op jit(solution)/shard_map/ppermute | solution.py:336
  49.5 55.5 %collective-permute-start.10 = (bf16[3,1024,256]{2,1,0:T(8,128)(2,1)S(1)}, bf16[3,1024,256]{2,1,0:T(8,128)(2,1)S(1)}, u32[]{:S(2)}, u32[]{:S(2)}) collective-permute-start(bf16[3,1024,256]{2,1,0:T(8,128)(2,1)S(1)} %get-tuple-element.29.refs_0_.refs_12_), channel_id=1, source_target_pairs={{0,16},{4,20},{8,24},{12,28},{16,0},{20,4},{24,8},{28,12},{1,17},{... | collective-permute-start | bytes 4718600 | tf_op jit(solution)/shard_map/ppermute | solution.py:336
  64.4 16.6 %collective-permute-start.4 = (bf16[3,512,256]{2,1,0:T(8,128)(2,1)}, bf16[3,512,256]{2,1,0:T(8,128)(2,1)S(1)}, u32[]{:S(2)}, u32[]{:S(2)}) collective-permute-start(bf16[3,512,256]{2,1,0:T(8,128)(2,1)} %collective-permute-done.1.refs_0_.refs_8_), channel_id=1, source_target_pairs={{0,4},{4,0},{8,12},{12,8},{16,20},{20,16},{24,28},{28,24},{1,5},{5... | collective-permute-start | bytes 2359304 | tf_op jit(solution)/shard_map/ppermute | solution.py:336
  68.1 13.0 %collective-permute-start.5 = (bf16[3,512,256]{2,1,0:T(8,128)(2,1)}, bf16[3,512,256]{2,1,0:T(8,128)(2,1)S(1)}, u32[]{:S(2)}, u32[]{:S(2)}) collective-permute-start(bf16[3,512,256]{2,1,0:T(8,128)(2,1)} %collective-permute-done.3.refs_1_.refs_9_), channel_id=1, source_target_pairs={{0,4},{4,0},{8,12},{12,8},{16,20},{20,16},{24,28},{28,24},{1,5},{5... | collective-permute-start | bytes 2359304 | tf_op jit(solution)/shard_map/ppermute | solution.py:336
  69.2 42.1 %collective-permute-start.13 = (bf16[3,1024,256]{2,1,0:T(8,128)(2,1)S(1)}, bf16[3,1024,256]{2,1,0:T(8,128)(2,1)S(1)}, u32[]{:S(2)}, u32[]{:S(2)}) collective-permute-start(bf16[3,1024,256]{2,1,0:T(8,128)(2,1)S(1)} %get-tuple-element.29.refs_0_.refs_12_), channel_id=1, source_target_pairs={{0,4},{4,0},{8,12},{12,8},{16,20},{20,16},{24,28},{28,24},{1,5},{5... | collective-permute-start | bytes 4718600 | tf_op jit(solution)/shard_map/ppermute | solution.py:336
  81.1 6.5 %copy-start.6 = (bf16[3,512,256]{2,1,0:T(8,128)(2,1)}, bf16[3,512,256]{2,1,0:T(8,128)(2,1)S(1)}, u32[]{:S(2)}) copy-start(bf16[3,512,256]{2,1,0:T(8,128)(2,1)S(1)} %collective-permute-done.4.refs_2_.refs_10_) | copy-start | bytes 2359300
  81.1 6.5 %copy-start.8 = (bf16[3,512,256]{2,1,0:T(8,128)(2,1)}, bf16[3,512,256]{2,1,0:T(8,128)(2,1)S(1)}, u32[]{:S(2)}) copy-start(bf16[3,512,256]{2,1,0:T(8,128)(2,1)S(1)} %collective-permute-done.5.refs_3_.refs_11_) | copy-start | bytes 2359300
  87.6 19.7 %copy-start.31 = (f32[512]{0:T(512)S(1)}, f32[512]{0:T(512)}, u32[]{:S(2)}) copy-start(f32[512]{0:T(512)} %param.11) | copy-start | bytes 6148
  104.6 6.7 %copy-start.2 = (bf16[3,1024,256]{2,1,0:T(8,128)(2,1)}, bf16[3,1024,256]{2,1,0:T(8,128)(2,1)S(1)}, u32[]{:S(2)}) copy-start(bf16[3,1024,256]{2,1,0:T(8,128)(2,1)S(1)} %collective-permute-done.9.refs_2_.refs_14_) | copy-start | bytes 4718596
  104.6 6.8 %collective-permute-start.14 = (bf16[3,1024,256]{2,1,0:T(8,128)(2,1)S(1)}, bf16[3,1024,256]{2,1,0:T(8,128)(2,1)S(1)}, u32[]{:S(2)}, u32[]{:S(2)}) collective-permute-start(bf16[3,1024,256]{2,1,0:T(8,128)(2,1)S(1)} %collective-permute-done.9.refs_2_.refs_14_), channel_id=1, source_target_pairs={{0,4},{4,0},{8,12},{12,8},{16,20},{20,16},{24,28},{28,24},{1,5},{5... | collective-permute-start | bytes 4718600 | tf_op jit(solution)/shard_map/ppermute | solution.py:336
  105.0 6.3 %copy-start.19 = (bf16[3,1024,256]{2,1,0:T(8,128)(2,1)}, bf16[3,1024,256]{2,1,0:T(8,128)(2,1)S(1)}, u32[]{:S(2)}) copy-start(bf16[3,1024,256]{2,1,0:T(8,128)(2,1)S(1)} %collective-permute-done.10.refs_4_.refs_16_) | copy-start | bytes 4718596
  105.0 6.4 %collective-permute-start.15 = (bf16[3,1024,256]{2,1,0:T(8,128)(2,1)S(1)}, bf16[3,1024,256]{2,1,0:T(8,128)(2,1)}, u32[]{:S(2)}, u32[]{:S(2)}) collective-permute-start(bf16[3,1024,256]{2,1,0:T(8,128)(2,1)S(1)} %collective-permute-done.10.refs_4_.refs_16_), channel_id=1, source_target_pairs={{0,4},{4,0},{8,12},{12,8},{16,20},{20,16},{24,28},{28,24},{1,5},{5... | collective-permute-start | bytes 4718600 | tf_op jit(solution)/shard_map/ppermute | solution.py:336
  105.2 20.0 %collective-permute-start.11 = (bf16[3,512,256]{2,1,0:T(8,128)(2,1)S(1)}, bf16[3,512,256]{2,1,0:T(8,128)(2,1)}, u32[]{:S(2)}, u32[]{:S(2)}) collective-permute-start(bf16[3,512,256]{2,1,0:T(8,128)(2,1)S(1)} %slice.109), channel_id=1, source_target_pairs={{0,16},{4,20},{8,24},{12,28},{16,0},{20,4},{24,8},{28,12},{1,17},{... | collective-permute-start | bytes 2359304 | tf_op jit(solution)/shard_map/ppermute | solution.py:336
  106.8 19.7 %collective-permute-start.12 = (bf16[3,512,256]{2,1,0:T(8,128)(2,1)S(1)}, bf16[3,512,256]{2,1,0:T(8,128)(2,1)}, u32[]{:S(2)}, u32[]{:S(2)}) collective-permute-start(bf16[3,512,256]{2,1,0:T(8,128)(2,1)S(1)} %slice.110), channel_id=1, source_target_pairs={{0,8},{4,12},{8,0},{12,4},{16,24},{20,28},{24,16},{28,20},{1,9},{5... | collective-permute-start | bytes 2359304 | tf_op jit(solution)/shard_map/ppermute | solution.py:336
  111.3 10.9 %copy-start.10 = (bf16[512,768]{1,0:T(8,128)(2,1)}, bf16[512,768]{1,0:T(8,128)(2,1)S(1)}, u32[]{:S(2)}) copy-start(bf16[512,768]{1,0:T(8,128)(2,1)S(1)} %get-tuple-element.34.refs_0_) | copy-start | bytes 2359300
  111.3 10.9 %copy-start.15 = (bf16[512,256]{1,0:T(8,128)(2,1)}, bf16[512,256]{1,0:T(8,128)(2,1)S(1)}, u32[]{:S(2)}) copy-start(bf16[512,256]{1,0:T(8,128)(2,1)S(1)} %get-tuple-element.28) | copy-start | bytes 786436
  111.3 10.9 %copy-start.4 = (bf16[3,1024,256]{2,1,0:T(8,128)(2,1)}, bf16[3,1024,256]{2,1,0:T(8,128)(2,1)S(1)}, u32[]{:S(2)}) copy-start(bf16[3,1024,256]{2,1,0:T(8,128)(2,1)S(1)} %collective-permute-done.13.refs_1_.refs_13_) | copy-start | bytes 4718596
  111.4 1.2 copy-start.20
  122.3 1.2 copy-start.13
  126.5 2.6 collective-permute-start.16
  126.5 3.7 %collective-permute-start.17 = (bf16[3,512,256]{2,1,0:T(8,128)(2,1)}, bf16[3,512,256]{2,1,0:T(8,128)(2,1)}, u32[]{:S(2)}, u32[]{:S(2)}) collective-permute-start(bf16[3,512,256]{2,1,0:T(8,128)(2,1)} %collective-permute-done.12.refs_1_.refs_19_), channel_id=1, source_target_pairs={{0,4},{4,0},{8,12},{12,8},{16,20},{20,16},{24,28},{28,24},{1,5},{5... | collective-permute-start | bytes 2359304 | tf_op jit(solution)/shard_map/ppermute | solution.py:336
  130.2 1.4 copy-start.14
  131.7 19.6 %copy-start.5 = (bf16[3,1024,256]{2,1,0:T(8,128)(2,1)S(1)}, bf16[3,1024,256]{2,1,0:T(8,128)(2,1)}, u32[]{:S(2)}) copy-start(bf16[3,1024,256]{2,1,0:T(8,128)(2,1)} %copy-done.4) | copy-start | bytes 4718596
  131.7 19.6 %copy-start.7 = (bf16[3,512,256]{2,1,0:T(8,128)(2,1)S(1)}, bf16[3,512,256]{2,1,0:T(8,128)(2,1)}, u32[]{:S(2)}) copy-start(bf16[3,512,256]{2,1,0:T(8,128)(2,1)} %copy-done.6) | copy-start | bytes 2359300
  131.7 19.6 %copy-start.9 = (bf16[3,512,256]{2,1,0:T(8,128)(2,1)S(1)}, bf16[3,512,256]{2,1,0:T(8,128)(2,1)}, u32[]{:S(2)}) copy-start(bf16[3,512,256]{2,1,0:T(8,128)(2,1)} %copy-done.8) | copy-start | bytes 2359300
  131.7 19.6 %copy-start.11 = (bf16[512,768]{1,0:T(8,128)(2,1)S(1)}, bf16[512,768]{1,0:T(8,128)(2,1)}, u32[]{:S(2)}) copy-start(bf16[512,768]{1,0:T(8,128)(2,1)} %copy-done.10) | copy-start | bytes 2359300
  138.8 12.5 %copy-start.3 = (bf16[3,1024,256]{2,1,0:T(8,128)(2,1)S(1)}, bf16[3,1024,256]{2,1,0:T(8,128)(2,1)}, u32[]{:S(2)}) copy-start(bf16[3,1024,256]{2,1,0:T(8,128)(2,1)} %copy-done.2) | copy-start | bytes 4718596
  151.3 3.8 %copy-start.17 = (bf16[512,256]{1,0:T(8,128)(2,1)}, bf16[512,256]{1,0:T(8,128)(2,1)S(1)}, u32[]{:S(2)}) copy-start(bf16[512,256]{1,0:T(8,128)(2,1)S(1)} %get-tuple-element.40) | copy-start | bytes 786436
  151.3 8.1 %copy-start.12 = (bf16[512,768]{1,0:T(8,128)(2,1)}, bf16[512,768]{1,0:T(8,128)(2,1)S(1)}, u32[]{:S(2)}) copy-start(bf16[512,768]{1,0:T(8,128)(2,1)S(1)} %get-tuple-element.41.refs_1_) | copy-start | bytes 2359300
  155.1 16.8 %collective-permute-start.18 = (bf16[512,512]{1,0:T(8,128)(2,1)}, bf16[512,512]{1,0:T(8,128)(2,1)}, u32[]{:S(2)}, u32[]{:S(2)}) collective-permute-start(bf16[512,512]{1,0:T(8,128)(2,1)} %input_grad.12), channel_id=1, source_target_pairs={{0,1},{3,2},{4,5},{7,6},{8,9},{11,10},{12,13},{15,14},{16,17},{19,... | collective-permute-start | bytes 1572872 | tf_op jit(solution)/shard_map/ppermute | solution.py:474
  162.8 19.6 %collective-permute-start.19 = (bf16[512,512]{1,0:T(8,128)(2,1)}, bf16[512,512]{1,0:T(8,128)(2,1)S(1)}, u32[]{:S(2)}, u32[]{:S(2)}) collective-permute-start(bf16[512,512]{1,0:T(8,128)(2,1)} %input_grad.13), channel_id=1, source_target_pairs={{0,1},{3,2},{4,5},{7,6},{8,9},{11,10},{12,13},{15,14},{16,17},{19,... | collective-permute-start | bytes 1572872 | tf_op jit(solution)/shard_map/ppermute | solution.py:474
  170.5 34.4 %collective-permute-start.25 = (bf16[512,1024]{1,0:T(8,128)(2,1)}, bf16[512,1024]{1,0:T(8,128)(2,1)S(1)}, u32[]{:S(2)}, u32[]{:S(2)}) collective-permute-start(bf16[512,1024]{1,0:T(8,128)(2,1)} %input_grad.16), channel_id=1, source_target_pairs={{0,1},{3,2},{4,5},{7,6},{8,9},{11,10},{12,13},{15,14},{16,17},{19,... | collective-permute-start | bytes 3145736 | tf_op jit(solution)/shard_map/ppermute | solution.py:474
  184.0 48.5 %collective-permute-start.23 = (bf16[512,1024]{1,0:T(8,128)(2,1)S(1)}, bf16[512,1024]{1,0:T(8,128)(2,1)}, u32[]{:S(2)}, u32[]{:S(2)}) collective-permute-start(bf16[512,1024]{1,0:T(8,128)(2,1)S(1)} %add_convert_fusion.6), channel_id=1, source_target_pairs={{1,2},{2,1},{5,6},{6,5},{9,10},{10,9},{13,14},{14,13},{17,18},{18,... | collective-permute-start | bytes 3145736 | tf_op jit(solution)/shard_map/ppermute | solution.py:474
  187.6 17.3 %copy-start.23 = (bf16[512,1024]{1,0:T(8,128)(2,1)S(1)}, bf16[512,1024]{1,0:T(8,128)(2,1)}, u32[]{:S(2)}) copy-start(bf16[512,1024]{1,0:T(8,128)(2,1)} %input_grad.16) | copy-start | bytes 3145732
  194.0 43.0 %collective-permute-start.20 = (bf16[512,1024]{1,0:T(8,128)(2,1)}, bf16[512,1024]{1,0:T(8,128)(2,1)}, u32[]{:S(2)}, u32[]{:S(2)}) collective-permute-start(bf16[512,1024]{1,0:T(8,128)(2,1)} %input_grad.11), channel_id=1, source_target_pairs={{0,1},{3,2},{4,5},{7,6},{8,9},{11,10},{12,13},{15,14},{16,17},{19,... | collective-permute-start | bytes 3145736 | tf_op jit(solution)/shard_map/ppermute | solution.py:474
  206.4 43.9 %collective-permute-start.28 = (bf16[512,1024]{1,0:T(8,128)(2,1)}, bf16[512,1024]{1,0:T(8,128)(2,1)}, u32[]{:S(2)}, u32[]{:S(2)}) collective-permute-start(bf16[512,1024]{1,0:T(8,128)(2,1)} %add_convert_fusion.2), channel_id=1, source_target_pairs={{1,2},{2,1},{5,6},{6,5},{9,10},{10,9},{13,14},{14,13},{17,18},{18,... | collective-permute-start | bytes 3145736 | tf_op jit(solution)/shard_map/ppermute | solution.py:474
  220.6 33.7 %collective-permute-start.26 = (bf16[512,1024]{1,0:T(8,128)(2,1)}, bf16[512,1024]{1,0:T(8,128)(2,1)}, u32[]{:S(2)}, u32[]{:S(2)}) collective-permute-start(bf16[512,1024]{1,0:T(8,128)(2,1)} %input_grad.15), channel_id=1, source_target_pairs={{0,1},{3,2},{4,5},{7,6},{8,9},{11,10},{12,13},{15,14},{16,17},{19,... | collective-permute-start | bytes 3145736 | tf_op jit(solution)/shard_map/ppermute | solution.py:474
  232.5 4.5 %copy-start.26 = (bf16[512,1024]{1,0:T(8,128)(2,1)S(1)}, bf16[512,1024]{1,0:T(8,128)(2,1)}, u32[]{:S(2)}) copy-start(bf16[512,1024]{1,0:T(8,128)(2,1)} %input_grad.11) | copy-start | bytes 3145732
  235.6 5.9 %copy-start.22 = (bf16[512,1024]{1,0:T(8,128)(2,1)S(1)}, bf16[512,1024]{1,0:T(8,128)(2,1)}, u32[]{:S(2)}) copy-start(bf16[512,1024]{1,0:T(8,128)(2,1)} %input_grad.10) | copy-start | bytes 3145732
  235.6 14.7 %copy-start.21 = (bf16[512,1024]{1,0:T(8,128)(2,1)S(1)}, bf16[512,1024]{1,0:T(8,128)(2,1)}, u32[]{:S(2)}) copy-start(bf16[512,1024]{1,0:T(8,128)(2,1)} %input_grad.17) | copy-start | bytes 3145732
  235.6 36.6 %collective-permute-start.24 = (bf16[512,1024]{1,0:T(8,128)(2,1)}, bf16[512,1024]{1,0:T(8,128)(2,1)}, u32[]{:S(2)}, u32[]{:S(2)}) collective-permute-start(bf16[512,1024]{1,0:T(8,128)(2,1)} %add_convert_fusion.5), channel_id=1, source_target_pairs={{1,0},{2,3},{5,4},{6,7},{9,8},{10,11},{13,12},{14,15},{17,16},{18,... | collective-permute-start | bytes 3145736 | tf_op jit(solution)/shard_map/ppermute | solution.py:474
  239.6 14.7 %copy-start.25 = (bf16[512,1024]{1,0:T(8,128)(2,1)S(1)}, bf16[512,1024]{1,0:T(8,128)(2,1)}, u32[]{:S(2)}) copy-start(bf16[512,1024]{1,0:T(8,128)(2,1)} %input_grad.15) | copy-start | bytes 3145732
  239.6 38.5 %collective-permute-start.22 = (bf16[512,1024]{1,0:T(8,128)(2,1)}, bf16[512,1024]{1,0:T(8,128)(2,1)}, u32[]{:S(2)}, u32[]{:S(2)}) collective-permute-start(bf16[512,1024]{1,0:T(8,128)(2,1)} %add_convert_fusion.7), channel_id=1, source_target_pairs={{1,2},{2,1},{5,6},{6,5},{9,10},{10,9},{13,14},{14,13},{17,18},{18,... | collective-permute-start | bytes 3145736 | tf_op jit(solution)/shard_map/ppermute | solution.py:474
  241.4 38.2 %collective-permute-start.21 = (bf16[512,1024]{1,0:T(8,128)(2,1)S(1)}, bf16[512,1024]{1,0:T(8,128)(2,1)}, u32[]{:S(2)}, u32[]{:S(2)}) collective-permute-start(bf16[512,1024]{1,0:T(8,128)(2,1)S(1)} %copy-done.22), channel_id=1, source_target_pairs={{0,1},{3,2},{4,5},{7,6},{8,9},{11,10},{12,13},{15,14},{16,17},{19,... | collective-permute-start | bytes 3145736 | tf_op jit(solution)/shard_map/ppermute | solution.py:474
  252.9 5.7 %copy-start.16 = (bf16[512,256]{1,0:T(8,128)(2,1)S(1)}, bf16[512,256]{1,0:T(8,128)(2,1)}, u32[]{:S(2)}) copy-start(bf16[512,256]{1,0:T(8,128)(2,1)} %copy-done.15) | copy-start | bytes 786436
  252.9 5.7 %copy-start.18 = (bf16[512,256]{1,0:T(8,128)(2,1)S(1)}, bf16[512,256]{1,0:T(8,128)(2,1)}, u32[]{:S(2)}) copy-start(bf16[512,256]{1,0:T(8,128)(2,1)} %copy-done.17) | copy-start | bytes 786436
  252.9 32.8 %collective-permute-start.29 = (bf16[512,1024]{1,0:T(8,128)(2,1)}, bf16[512,1024]{1,0:T(8,128)(2,1)}, u32[]{:S(2)}, u32[]{:S(2)}) collective-permute-start(bf16[512,1024]{1,0:T(8,128)(2,1)} %add_convert_fusion.1), channel_id=1, source_target_pairs={{1,0},{2,3},{5,4},{6,7},{9,8},{10,11},{13,12},{14,15},{17,16},{18,... | collective-permute-start | bytes 3145736 | tf_op jit(solution)/shard_map/ppermute | solution.py:474
  257.0 28.7 %collective-permute-start.27 = (bf16[512,1024]{1,0:T(8,128)(2,1)}, bf16[512,1024]{1,0:T(8,128)(2,1)}, u32[]{:S(2)}, u32[]{:S(2)}) collective-permute-start(bf16[512,1024]{1,0:T(8,128)(2,1)} %add_convert_fusion.3), channel_id=1, source_target_pairs={{1,2},{2,1},{5,6},{6,5},{9,10},{10,9},{13,14},{14,13},{17,18},{18,... | collective-permute-start | bytes 3145736 | tf_op jit(solution)/shard_map/ppermute | solution.py:474
  272.1 7.6 %copy-start.24 = (bf16[512,1024]{1,0:T(8,128)(2,1)S(1)}, bf16[512,1024]{1,0:T(8,128)(2,1)}, u32[]{:S(2)}) copy-start(bf16[512,1024]{1,0:T(8,128)(2,1)} %input_grad.9) | copy-start | bytes 3145732
  272.2 18.3 %collective-permute-start.30 = (bf16[512,512]{1,0:T(8,128)(2,1)S(1)}, bf16[512,512]{1,0:T(8,128)(2,1)S(1)}, u32[]{:S(2)}, u32[]{:S(2)}) collective-permute-start(bf16[512,512]{1,0:T(8,128)(2,1)S(1)} %get-tuple-element.51), channel_id=1, source_target_pairs={{0,1},{3,2},{4,5},{7,6},{8,9},{11,10},{12,13},{15,14},{16,17},{19,... | collective-permute-start | bytes 1572872 | tf_op jit(solution)/shard_map/ppermute | solution.py:474
  278.2 7.5 %copy-start.27 = (bf16[512,1024]{1,0:T(8,128)(2,1)S(1)}, bf16[512,1024]{1,0:T(8,128)(2,1)}, u32[]{:S(2)}) copy-start(bf16[512,1024]{1,0:T(8,128)(2,1)} %input_grad.14) | copy-start | bytes 3145732
  278.2 21.4 %collective-permute-start.31 = (bf16[512,512]{1,0:T(8,128)(2,1)S(1)}, bf16[512,512]{1,0:T(8,128)(2,1)S(1)}, u32[]{:S(2)}, u32[]{:S(2)}) collective-permute-start(bf16[512,512]{1,0:T(8,128)(2,1)S(1)} %get-tuple-element.50), channel_id=1, source_target_pairs={{0,1},{3,2},{4,5},{7,6},{8,9},{11,10},{12,13},{15,14},{16,17},{19,... | collective-permute-start | bytes 1572872 | tf_op jit(solution)/shard_map/ppermute | solution.py:474
  299.8 1.3 copy-start.28
